TPU v7x, 256 devices: a whole 4x4x8 slice. The times are simulated.
256 devices in a mesh: seq: 32 (over z, y), head: 8 (over x, core).
Axes of the slice: x: 4, y: 4, z: 8, core: 2. Of those that a mesh axis runs over, the one named last changes fastest.
Arguments:
- q_data: bfloat16 [32768, 6144], P(('seq', 'head')), may hold values from -20 to 20
- k_data: bfloat16 [32768, 6144], P(('seq', 'head')), may hold values from -20 to 20
- v_data: bfloat16 [32768, 6144], P(('seq', 'head')), may hold values from -6 to 6
- q_exp: int32 [256, 48], P(('seq', 'head')), may hold values from -1 to 1
- k_exp: int32 [256, 48], P(('seq', 'head')), may hold values from -1 to 1
- v_exp: int32 [256, 48], P(('seq', 'head')), may hold values from -1 to 1
- extents: int32 [48, 3], replicated, may hold values from 0 to 3, as said below
Outputs:
- attended: bfloat16 [32768, 6144], P(('seq', 'head'))
Inputs may be any that keep to these rules, and one draw needn't show every extreme that they name: `extents`: column 0 is 0 or 1, column 1 at most 3, column 2 at most 1; some head has all three largest values.
All inputs are finite; a program needn't handle non-finite values.
Results may differ from a plain program's by a relative error of at most 0.0049.
Values may be sent and summed in bfloat16 or wider, within the bound.
A program may use at most 128 MiB of HBM per device.

v0:
```python
import math

import jax
import jax.numpy as jnp
from jax import lax
from jax.sharding import PartitionSpec as P

H = 48
HD = 128
TILE = 128
WT = 2


def padded(block, sides, width):
    for axis, dim in sides:
        count = lax.axis_size(axis)
        forward = [(i, i + 1) for i in range(count - 1)]
        backward = [(target, source) for source, target in forward]
        low = lax.ppermute(
            lax.slice_in_dim(block, block.shape[dim] - width, None, axis=dim), axis, forward
        )
        high = lax.ppermute(lax.slice_in_dim(block, 0, width, axis=dim), axis, backward)
        block = jnp.concatenate([low, block, high], axis=dim)
    return block


def allowed_pairs(extent, frame_index, frame_total, frame_tokens):
    row_index = jnp.arange(frame_tokens, dtype=jnp.int32)
    key_index = jnp.arange(3 * frame_tokens, dtype=jnp.int32)
    query_tile = row_index // TILE
    key_tile = key_index % frame_tokens // TILE
    frame_step = key_index // frame_tokens - 1
    near_frame = (
        (jnp.abs(frame_step) <= extent[0])
        & (frame_index + frame_step >= 0)
        & (frame_index + frame_step < frame_total)
    )
    near_height = jnp.abs(query_tile[:, None] // WT - key_tile[None, :] // WT) <= extent[1]
    near_width = jnp.abs(query_tile[:, None] % WT - key_tile[None, :] % WT) <= extent[2]
    return near_frame[None, :] & near_height & near_width


def attend_head(queries, keys_near, values_near, extent, frame_index, frame_total):
    frame_tokens = queries.shape[0]
    scores = lax.dot_general(
        queries, keys_near, (((1,), (1,)), ((), ())), preferred_element_type=jnp.float32
    )
    scores = scores * (1.0 / math.sqrt(queries.shape[1]))
    scores = jnp.where(allowed_pairs(extent, frame_index, frame_total, frame_tokens), scores, -1e30)
    peak = jnp.max(scores, axis=1, keepdims=True)
    weights = jnp.exp(scores - peak)
    weights = weights / jnp.sum(weights, axis=1, keepdims=True)
    return jnp.dot(
        weights.astype(jnp.bfloat16), values_near, preferred_element_type=jnp.float32
    ).astype(jnp.bfloat16)


def dequantize(data, exponents):
    tiles, head_count = exponents.shape
    scale = jnp.exp2(exponents.astype(jnp.float32)).astype(jnp.bfloat16)
    blocks = data.reshape(tiles, TILE, head_count, HD) * scale[:, None, :, None]
    return blocks.reshape(tiles * TILE, head_count, HD)


def attend_group(query_data, key_data, value_data, query_exp, key_exp, value_exp, extent):
    frame_index = lax.axis_index("seq")
    frame_total = lax.axis_size("seq")
    queries = dequantize(query_data, query_exp)
    keys_here = dequantize(key_data, key_exp)
    values_here = dequantize(value_data, value_exp)
    frame_tokens, head_count = (queries.shape[0], queries.shape[1])
    stacked = jnp.stack([keys_here, values_here])[:, None]
    rimmed = padded(stacked, (("seq", 1),), 1)
    keys_near = rimmed[0].reshape(3 * frame_tokens, head_count, HD)
    values_near = rimmed[1].reshape(3 * frame_tokens, head_count, HD)

    def one_head(pieces):
        return attend_head(pieces[0], pieces[1], pieces[2], pieces[3], frame_index, frame_total)

    result = lax.map(
        one_head,
        (
            jnp.moveaxis(queries, 1, 0),
            jnp.moveaxis(keys_near, 1, 0),
            jnp.moveaxis(values_near, 1, 0),
            extent,
        ),
    )
    return jnp.moveaxis(result, 0, 1)


def on_device(q_data, k_data, v_data, q_exp, k_exp, v_exp, extents):
    groups = lax.axis_size("head")
    local_tokens = q_data.shape[0]
    local_tiles = q_exp.shape[0]
    group_heads = H // groups
    query_wide = q_data.reshape(local_tokens, groups, group_heads * HD)
    key_wide = k_data.reshape(local_tokens, groups, group_heads * HD)
    value_wide = v_data.reshape(local_tokens, groups, group_heads * HD)
    query_scale = q_exp.reshape(local_tiles, groups, group_heads)
    key_scale = k_exp.reshape(local_tiles, groups, group_heads)
    value_scale = v_exp.reshape(local_tiles, groups, group_heads)
    received = (
        lax.all_to_all(query_wide, "head", split_axis=1, concat_axis=0, tiled=True),
        lax.all_to_all(key_wide, "head", split_axis=1, concat_axis=0, tiled=True),
        lax.all_to_all(value_wide, "head", split_axis=1, concat_axis=0, tiled=True),
        lax.all_to_all(query_scale, "head", split_axis=1, concat_axis=0, tiled=True),
        lax.all_to_all(key_scale, "head", split_axis=1, concat_axis=0, tiled=True),
        lax.all_to_all(value_scale, "head", split_axis=1, concat_axis=0, tiled=True),
    )
    frame_tokens = received[0].shape[0]
    frame_tiles = received[3].shape[0]
    extent = lax.dynamic_slice_in_dim(extents, lax.axis_index("head") * group_heads, group_heads, 0)
    result = attend_group(
        received[0].reshape(frame_tokens, group_heads, HD),
        received[1].reshape(frame_tokens, group_heads, HD),
        received[2].reshape(frame_tokens, group_heads, HD),
        received[3].reshape(frame_tiles, group_heads),
        received[4].reshape(frame_tiles, group_heads),
        received[5].reshape(frame_tiles, group_heads),
        extent,
    )
    returned = lax.all_to_all(
        result.reshape(frame_tokens, 1, group_heads * HD),
        "head",
        split_axis=0,
        concat_axis=1,
        tiled=True,
    )
    return returned.reshape(local_tokens, H * HD)


def solution(mesh):
    in_specs = (
        P(("seq", "head"), None),
        P(("seq", "head"), None),
        P(("seq", "head"), None),
        P(("seq", "head"), None),
        P(("seq", "head"), None),
        P(("seq", "head"), None),
        P(),
    )
    out_specs = P(("seq", "head"), None)
    return jax.shard_map(
        on_device, mesh=mesh, in_specs=in_specs, out_specs=out_specs, check_vma=False
    )
```

profile of v0, /device:TPU:1, one launch (start us, length us, event | category | flops | bytes accessed | tf_op | source)
XLA Modules:
  0.0 331.5 jit_solution(4022909998242004660)
XLA Ops:
  2.4 6.5 %all-to-all-start.5 = ((s32[1,8,6]{2,0,1:T(1,128)}), s32[1,8,6]{2,0,1:T(1,128)S(1)}, u32[]{:S(2)}, u32[]{:S(2)}) async-start(s32[1,8,6]{2,0,1:T(1,128)} %bitcast.23), calls=%async_computation.5 | async-start | bytes 8192 | tf_op jit(solution)/shard_map/all_to_all | solution.py:109
  10.8 2.6 all-to-all-done.5
  13.4 3.8 %all-to-all-start.3 = ((s32[1,8,6]{2,0,1:T(1,128)}), s32[1,8,6]{2,0,1:T(1,128)S(1)}, u32[]{:S(2)}, u32[]{:S(2)}) async-start(s32[1,8,6]{2,0,1:T(1,128)} %bitcast.17), calls=%async_computation.3 | async-start | bytes 8192 | tf_op jit(solution)/shard_map/all_to_all | solution.py:108
  17.2 2.7 copy.38
  19.9 1.9 all-to-all-done.3
  21.8 4.2 %all-to-all-start.2 = ((bf16[128,8,768]{0,2,1:T(8,128)(2,1)}), bf16[128,8,768]{0,2,1:T(8,128)(2,1)S(1)}, u32[]{:S(2)}, u32[]{:S(2)}) async-start(bf16[128,8,768]{0,2,1:T(8,128)(2,1)} %bitcast.14), calls=%async_computation.2 | async-start | bytes 3145728 | tf_op jit(solution)/shard_map/all_to_all | solution.py:105
  27.5 19.2 %all-to-all-done.2 = bf16[128,8,768]{0,2,1:T(8,128)(2,1)S(1)} async-done(((bf16[128,8,768]{0,2,1:T(8,128)(2,1)}), bf16[128,8,768]{0,2,1:T(8,128)(2,1)S(1)}, u32[]{:S(2)}, u32[]{:S(2)}) %all-to-all-start.2) | async-done | bytes 1572896 | tf_op jit(solution)/shard_map/all_to_all | solution.py:105
  46.7 4.4 %all-to-all-start.4 = ((bf16[128,8,768]{0,2,1:T(8,128)(2,1)}), bf16[128,8,768]{0,2,1:T(8,128)(2,1)S(1)}, u32[]{:S(2)}, u32[]{:S(2)}) async-start(bf16[128,8,768]{0,2,1:T(8,128)(2,1)} %bitcast.20), calls=%async_computation.4 | async-start | bytes 3145728 | tf_op jit(solution)/shard_map/all_to_all | solution.py:106
  51.5 2.2 copy.39
  53.6 3.7 %reshape_reshape.10 = bf16[1,1024,6,128]{1,3,2,0:T(8,128)(2,1)} reshape(bf16[8,128,1,768]{1,0,3,2:T(8,128)(2,1)} %copy.39) | data formatting | bytes 3145728 | tf_op jit(solution)/shard_map/reshape;reshape | solution.py:61
  57.3 14.5 %all-to-all-done.4 = bf16[128,8,768]{0,2,1:T(8,128)(2,1)S(1)} async-done(((bf16[128,8,768]{0,2,1:T(8,128)(2,1)}), bf16[128,8,768]{0,2,1:T(8,128)(2,1)S(1)}, u32[]{:S(2)}, u32[]{:S(2)}) %all-to-all-start.4) | async-done | bytes 1572896 | tf_op jit(solution)/shard_map/all_to_all | solution.py:106
  72.8 2.1 reshape_reshape.11
  76.9 4.2 %collective-permute-start = (bf16[2,1,1024,6,128]{2,4,3,0,1:T(8,128)(2,1)S(1)}, bf16[2,1,1024,6,128]{2,4,3,0,1:T(8,128)(2,1)}, u32[]{:S(2)}, u32[]{:S(2)}) collective-permute-start(bf16[2,1,1024,6,128]{2,4,3,0,1:T(8,128)(2,1)S(1)} %maximum_bitcast_fusion), channel_id=1, source_target_pairs={{0,8},{8,16},{16,24},{24,32},{32,40},{40,48},{48,56},{56,64},{64,7... | collective-permute-start | bytes 9437192 | tf_op jit(solution)/shard_map/ppermute | solution.py:19
  83.7 4.4 %all-to-all-start.1 = ((s32[1,8,6]{2,0,1:T(1,128)}), s32[1,8,6]{2,0,1:T(1,128)S(1)}, u32[]{:S(2)}, u32[]{:S(2)}) async-start(s32[1,8,6]{2,0,1:T(1,128)} %bitcast.10), calls=%async_computation.1 | async-start | bytes 8192 | tf_op jit(solution)/shard_map/all_to_all | solution.py:107
  88.0 2.6 copy.33
  90.6 1.9 all-to-all-done.1
  92.5 4.9 %all-to-all-start = ((bf16[128,8,768]{0,2,1:T(8,128)(2,1)}), bf16[128,8,768]{0,2,1:T(8,128)(2,1)}, u32[]{:S(2)}, u32[]{:S(2)}) async-start(bf16[128,8,768]{0,2,1:T(8,128)(2,1)} %bitcast.107), calls=%async_computation | async-start | bytes 3145728 | tf_op jit(solution)/shard_map/all_to_all | solution.py:104
  97.7 20.6 %all-to-all-done = bf16[128,8,768]{0,2,1:T(8,128)(2,1)} async-done(((bf16[128,8,768]{0,2,1:T(8,128)(2,1)}), bf16[128,8,768]{0,2,1:T(8,128)(2,1)}, u32[]{:S(2)}, u32[]{:S(2)}) %all-to-all-start) | async-done | bytes 1572896 | tf_op jit(solution)/shard_map/all_to_all | solution.py:104
  118.3 3.6 %copy.34 = bf16[8,128,1,768]{1,0,3,2:T(8,128)(2,1)} copy(bf16[8,128,1,768]{1,3,0,2:T(8,128)(2,1)} %bitcast.9) | data formatting | bytes 3145728 | tf_op jit(solution)/shard_map/all_to_all | solution.py:104
  121.8 3.7 %reshape_reshape.9 = bf16[1024,6,128]{0,2,1:T(8,128)(2,1)} reshape(bf16[8,128,1,768]{1,0,3,2:T(8,128)(2,1)} %copy.34) | data formatting | bytes 3145728 | tf_op jit(solution)/shard_map/reshape;reshape | solution.py:61
  125.5 2.7 multiply_bitcast_fusion
  128.2 17.8 %collective-permute-done = bf16[2,1,1024,6,128]{2,4,3,0,1:T(8,128)(2,1)} collective-permute-done((bf16[2,1,1024,6,128]{2,4,3,0,1:T(8,128)(2,1)S(1)}, bf16[2,1,1024,6,128]{2,4,3,0,1:T(8,128)(2,1)}, u32[]{:S(2)}, u32[]{:S(2)}) %collective-permute-start) | collective-permute-done | bytes 3145760 | tf_op jit(solution)/shard_map/ppermute | solution.py:19
  146.0 5.5 %collective-permute-done.1 = bf16[2,1,1024,6,128]{2,4,3,0,1:T(8,128)(2,1)} collective-permute-done((bf16[2,1,1024,6,128]{2,4,3,0,1:T(8,128)(2,1)S(1)}, bf16[2,1,1024,6,128]{2,4,3,0,1:T(8,128)(2,1)}, u32[]{:S(2)}, u32[]{:S(2)}) %collective-permute-start.1) | collective-permute-done | bytes 3145760 | tf_op jit(solution)/shard_map/ppermute | solution.py:22
  151.5 7.0 %pad_maximum_fusion = bf16[2,3,1024,6,128]{2,4,3,0,1:T(8,128)(2,1)} fusion(bf16[2,1,1024,6,128]{2,4,3,0,1:T(8,128)(2,1)} %collective-permute-done.1, bf16[2,1,1024,6,128]{2,4,3,0,1:T(8,128)(2,1)S(1)} %maximum_bitcast_fusion, bf16[2,1,1024,6,128]{2,4,3,0,1:T(8,128)(2,1)} %collective-permute-done), kind=kLoop, calls=%fused_computation.74 | loop fusion | flops 9437184 | bytes 18874368 | tf_op jit(solution)/shard_map/concatenate | solution.py:23
  158.5 9.3 %fusion.49 = (bf16[1,3,1024,6,128]{2,4,3,0,1:T(8,128)(2,1)}, bf16[1,3,1024,6,128]{2,4,3,0,1:T(8,128)(2,1)}) fusion(bf16[2,3,1024,6,128]{2,4,3,0,1:T(8,128)(2,1)} %pad_maximum_fusion), kind=kLoop, calls=%fused_computation.94 | loop fusion | bytes 18874368 | tf_op jit(solution)/shard_map/slice | solution.py:75
  167.8 6.6 %copy.48 = bf16[1,3,1024,6,128]{4,2,1,3,0:T(8,128)(2,1)} copy(bf16[1,3,1024,6,128]{2,4,3,0,1:T(8,128)(2,1)} %get-tuple-element.183) | data formatting | bytes 9437184 | tf_op jit(solution)/shard_map/slice | solution.py:74
  174.4 6.9 %copy.49 = bf16[1,3,1024,6,128]{4,2,1,3,0:T(8,128)(2,1)} copy(bf16[1,3,1024,6,128]{2,4,3,0,1:T(8,128)(2,1)} %get-tuple-element.182) | data formatting | bytes 9437184 | tf_op jit(solution)/shard_map/slice | solution.py:75
  181.3 108.5 %while.13 = (s32[]{:T(128)}, bf16[6,1024,128]{1,2,0:T(8,128)(2,1)S(1)}, s32[6,3]{0,1:T(4,128)S(1)}, s32[]{:T(128)}, bf16[6,1024,128]{1,2,0:T(8,128)(2,1)}, /*ind...) while((s32[]{:T(128)}, bf16[6,1024,128]{1,2,0:T(8,128)(2,1)S(1)}, ...), condition=%wide.region_3.4_spmd, body=%wide.region_0.3_spmd.sunk | while | flops 1661273088 | bytes 40989332 | solution.py:80
  182.6 10.9 %fusion.59 = (f32[1024]{0:T(1024)S(1)}, f32[1024,3072]{1,0:T(8,128)S(1)}) fusion(bf16[6,3072,128]{2,1,0:T(8,128)(2,1)} %get-tuple-element.268, s32[]{:T(128)} %get-tuple-element.255, bf16[6,1024,128]{1,2,0:T(8,128)(2,1)} %get-tuple-element.267, s32[]{:T(128)} %bitcast.104, s32[3072]{0:T(1024)S(1)} %get-tuple-element.239, ...), kind=kOutput, calls=%fused_computation.93.clone.1 | convolution fusion | flops 839908352 | bytes 13673472 | tf_op jit(solution)/shard_map/while/body/eval_jaxpr/dot_general | solution.py:45
  193.6 1.9 fusion.60
  195.4 3.7 %fusion.61 = bf16[1,1024,128]{2,1,0:T(8,128)(2,1)S(1)} fusion(f32[1024,3072]{1,0:T(8,128)S(1)} %get-tuple-element.245, f32[1024]{0:T(1024)S(1)} %fusion.60, f32[1024]{0:T(1024)S(1)} %get-tuple-element.246, bf16[6,3072,128]{2,1,0:T(8,128)(2,1)} %get-tuple-element.269, s32[]{:T(128)} %get-tuple-element.255), kind=kOutput, calls=%fused_computation.10.clone.1 | convolution fusion | flops 814874624 | bytes 13640192 | tf_op jit(solution)/shard_map/while/body/eval_jaxpr/dot_general | solution.py:53
  200.7 10.9 %fusion.59 = (f32[1024]{0:T(1024)S(1)}, f32[1024,3072]{1,0:T(8,128)S(1)}) fusion(bf16[6,3072,128]{2,1,0:T(8,128)(2,1)} %get-tuple-element.268, s32[]{:T(128)} %get-tuple-element.255, bf16[6,1024,128]{1,2,0:T(8,128)(2,1)} %get-tuple-element.267, s32[]{:T(128)} %bitcast.104, s32[3072]{0:T(1024)S(1)} %get-tuple-element.239, ...), kind=kOutput, calls=%fused_computation.93.clone.1 | convolution fusion | flops 839908352 | bytes 13673472 | tf_op jit(solution)/shard_map/while/body/eval_jaxpr/dot_general | solution.py:45
  211.6 1.9 fusion.60
  213.5 3.7 %fusion.61 = bf16[1,1024,128]{2,1,0:T(8,128)(2,1)S(1)} fusion(f32[1024,3072]{1,0:T(8,128)S(1)} %get-tuple-element.245, f32[1024]{0:T(1024)S(1)} %fusion.60, f32[1024]{0:T(1024)S(1)} %get-tuple-element.246, bf16[6,3072,128]{2,1,0:T(8,128)(2,1)} %get-tuple-element.269, s32[]{:T(128)} %get-tuple-element.255), kind=kOutput, calls=%fused_computation.10.clone.1 | convolution fusion | flops 814874624 | bytes 13640192 | tf_op jit(solution)/shard_map/while/body/eval_jaxpr/dot_general | solution.py:53
  218.8 10.9 %fusion.59 = (f32[1024]{0:T(1024)S(1)}, f32[1024,3072]{1,0:T(8,128)S(1)}) fusion(bf16[6,3072,128]{2,1,0:T(8,128)(2,1)} %get-tuple-element.268, s32[]{:T(128)} %get-tuple-element.255, bf16[6,1024,128]{1,2,0:T(8,128)(2,1)} %get-tuple-element.267, s32[]{:T(128)} %bitcast.104, s32[3072]{0:T(1024)S(1)} %get-tuple-element.239, ...), kind=kOutput, calls=%fused_computation.93.clone.1 | convolution fusion | flops 839908352 | bytes 13673472 | tf_op jit(solution)/shard_map/while/body/eval_jaxpr/dot_general | solution.py:45
  229.7 1.9 fusion.60
  231.5 3.7 %fusion.61 = bf16[1,1024,128]{2,1,0:T(8,128)(2,1)S(1)} fusion(f32[1024,3072]{1,0:T(8,128)S(1)} %get-tuple-element.245, f32[1024]{0:T(1024)S(1)} %fusion.60, f32[1024]{0:T(1024)S(1)} %get-tuple-element.246, bf16[6,3072,128]{2,1,0:T(8,128)(2,1)} %get-tuple-element.269, s32[]{:T(128)} %get-tuple-element.255), kind=kOutput, calls=%fused_computation.10.clone.1 | convolution fusion | flops 814874624 | bytes 13640192 | tf_op jit(solution)/shard_map/while/body/eval_jaxpr/dot_general | solution.py:53
  236.8 10.9 %fusion.59 = (f32[1024]{0:T(1024)S(1)}, f32[1024,3072]{1,0:T(8,128)S(1)}) fusion(bf16[6,3072,128]{2,1,0:T(8,128)(2,1)} %get-tuple-element.268, s32[]{:T(128)} %get-tuple-element.255, bf16[6,1024,128]{1,2,0:T(8,128)(2,1)} %get-tuple-element.267, s32[]{:T(128)} %bitcast.104, s32[3072]{0:T(1024)S(1)} %get-tuple-element.239, ...), kind=kOutput, calls=%fused_computation.93.clone.1 | convolution fusion | flops 839908352 | bytes 13673472 | tf_op jit(solution)/shard_map/while/body/eval_jaxpr/dot_general | solution.py:45
  247.7 1.9 fusion.60
  249.6 3.7 %fusion.61 = bf16[1,1024,128]{2,1,0:T(8,128)(2,1)S(1)} fusion(f32[1024,3072]{1,0:T(8,128)S(1)} %get-tuple-element.245, f32[1024]{0:T(1024)S(1)} %fusion.60, f32[1024]{0:T(1024)S(1)} %get-tuple-element.246, bf16[6,3072,128]{2,1,0:T(8,128)(2,1)} %get-tuple-element.269, s32[]{:T(128)} %get-tuple-element.255), kind=kOutput, calls=%fused_computation.10.clone.1 | convolution fusion | flops 814874624 | bytes 13640192 | tf_op jit(solution)/shard_map/while/body/eval_jaxpr/dot_general | solution.py:53
  254.9 10.9 %fusion.59 = (f32[1024]{0:T(1024)S(1)}, f32[1024,3072]{1,0:T(8,128)S(1)}) fusion(bf16[6,3072,128]{2,1,0:T(8,128)(2,1)} %get-tuple-element.268, s32[]{:T(128)} %get-tuple-element.255, bf16[6,1024,128]{1,2,0:T(8,128)(2,1)} %get-tuple-element.267, s32[]{:T(128)} %bitcast.104, s32[3072]{0:T(1024)S(1)} %get-tuple-element.239, ...), kind=kOutput, calls=%fused_computation.93.clone.1 | convolution fusion | flops 839908352 | bytes 13673472 | tf_op jit(solution)/shard_map/while/body/eval_jaxpr/dot_general | solution.py:45
  267.6 3.7 %fusion.61 = bf16[1,1024,128]{2,1,0:T(8,128)(2,1)S(1)} fusion(f32[1024,3072]{1,0:T(8,128)S(1)} %get-tuple-element.245, f32[1024]{0:T(1024)S(1)} %fusion.60, f32[1024]{0:T(1024)S(1)} %get-tuple-element.246, bf16[6,3072,128]{2,1,0:T(8,128)(2,1)} %get-tuple-element.269, s32[]{:T(128)} %get-tuple-element.255), kind=kOutput, calls=%fused_computation.10.clone.1 | convolution fusion | flops 814874624 | bytes 13640192 | tf_op jit(solution)/shard_map/while/body/eval_jaxpr/dot_general | solution.py:53
  272.9 10.9 %fusion.59 = (f32[1024]{0:T(1024)S(1)}, f32[1024,3072]{1,0:T(8,128)S(1)}) fusion(bf16[6,3072,128]{2,1,0:T(8,128)(2,1)} %get-tuple-element.268, s32[]{:T(128)} %get-tuple-element.255, bf16[6,1024,128]{1,2,0:T(8,128)(2,1)} %get-tuple-element.267, s32[]{:T(128)} %bitcast.104, s32[3072]{0:T(1024)S(1)} %get-tuple-element.239, ...), kind=kOutput, calls=%fused_computation.93.clone.1 | convolution fusion | flops 839908352 | bytes 13673472 | tf_op jit(solution)/shard_map/while/body/eval_jaxpr/dot_general | solution.py:45
  285.7 3.7 %fusion.61 = bf16[1,1024,128]{2,1,0:T(8,128)(2,1)S(1)} fusion(f32[1024,3072]{1,0:T(8,128)S(1)} %get-tuple-element.245, f32[1024]{0:T(1024)S(1)} %fusion.60, f32[1024]{0:T(1024)S(1)} %get-tuple-element.246, bf16[6,3072,128]{2,1,0:T(8,128)(2,1)} %get-tuple-element.269, s32[]{:T(128)} %get-tuple-element.255), kind=kOutput, calls=%fused_computation.10.clone.1 | convolution fusion | flops 814874624 | bytes 13640192 | tf_op jit(solution)/shard_map/while/body/eval_jaxpr/dot_general | solution.py:53
  291.5 3.3 reduce.12
  296.0 26.0 %all_to_all.87 = bf16[8,2,49152]{2,1,0:T(2,128)(2,1)} all-to-all(bf16[8,2,49152]{2,1,0:T(2,128)(2,1)S(1)} %reshape.298), channel_id=1, replica_groups=mesh['seq'=32,'head'=8] {'head'}, dimensions={0} | all-to-all | bytes 3145728 | tf_op jit(solution)/shard_map/all_to_all | solution.py:123
  321.9 4.7 %reshape.299 = bf16[1024,1,768]{2,1,0:T(2,128)(2,1)S(1)} reshape(bf16[8,2,49152]{2,1,0:T(2,128)(2,1)} %all_to_all.87) | data formatting | bytes 3145728
  328.0 1.9 copy.53
  (89 shorter events, 30.7 us)
Async XLA Ops:
  0.0 97.4 %copy-start = (s32[48,3]{0,1:T(4,128)S(1)}, s32[48,3]{0,1:T(4,128)}, u32[]{:S(2)}) copy-start(s32[48,3]{0,1:T(4,128)} %param.15) | copy-start | bytes 1732
  2.4 11.0 %all-to-all-start.5 = ((s32[1,8,6]{2,0,1:T(1,128)}), s32[1,8,6]{2,0,1:T(1,128)S(1)}, u32[]{:S(2)}, u32[]{:S(2)}) async-start(s32[1,8,6]{2,0,1:T(1,128)} %bitcast.23), calls=%async_computation.5 | async-start | bytes 8192 | tf_op jit(solution)/shard_map/all_to_all | solution.py:109
  13.4 8.4 %all-to-all-start.3 = ((s32[1,8,6]{2,0,1:T(1,128)}), s32[1,8,6]{2,0,1:T(1,128)S(1)}, u32[]{:S(2)}, u32[]{:S(2)}) async-start(s32[1,8,6]{2,0,1:T(1,128)} %bitcast.17), calls=%async_computation.3 | async-start | bytes 8192 | tf_op jit(solution)/shard_map/all_to_all | solution.py:108
  17.2 8.8 %copy-start.3 = (bf16[128,6144]{1,0:T(8,128)(2,1)S(1)}, bf16[128,6144]{1,0:T(8,128)(2,1)}, u32[]{:S(2)}) copy-start(bf16[128,6144]{1,0:T(8,128)(2,1)} %param.11) | copy-start | bytes 4718596
  21.8 24.9 %all-to-all-start.2 = ((bf16[128,8,768]{0,2,1:T(8,128)(2,1)}), bf16[128,8,768]{0,2,1:T(8,128)(2,1)S(1)}, u32[]{:S(2)}, u32[]{:S(2)}) async-start(bf16[128,8,768]{0,2,1:T(8,128)(2,1)} %bitcast.14), calls=%async_computation.2 | async-start | bytes 3145728 | tf_op jit(solution)/shard_map/all_to_all | solution.py:105
  46.7 25.1 %all-to-all-start.4 = ((bf16[128,8,768]{0,2,1:T(8,128)(2,1)}), bf16[128,8,768]{0,2,1:T(8,128)(2,1)S(1)}, u32[]{:S(2)}, u32[]{:S(2)}) async-start(bf16[128,8,768]{0,2,1:T(8,128)(2,1)} %bitcast.20), calls=%async_computation.4 | async-start | bytes 3145728 | tf_op jit(solution)/shard_map/all_to_all | solution.py:106
  72.8 2.1 copy-start.2
  76.6 5.8 %copy-start.6 = (s32[1,48]{1,0:T(1,128)S(1)}, s32[1,48]{1,0:T(1,128)}, u32[]{:S(2)}) copy-start(s32[1,48]{1,0:T(1,128)} %param.12) | copy-start | bytes 580
  76.9 69.1 %collective-permute-start = (bf16[2,1,1024,6,128]{2,4,3,0,1:T(8,128)(2,1)S(1)}, bf16[2,1,1024,6,128]{2,4,3,0,1:T(8,128)(2,1)}, u32[]{:S(2)}, u32[]{:S(2)}) collective-permute-start(bf16[2,1,1024,6,128]{2,4,3,0,1:T(8,128)(2,1)S(1)} %maximum_bitcast_fusion), channel_id=1, source_target_pairs={{0,8},{8,16},{16,24},{24,32},{32,40},{40,48},{48,56},{56,64},{64,7... | collective-permute-start | bytes 9437192 | tf_op jit(solution)/shard_map/ppermute | solution.py:19
  81.1 70.4 %collective-permute-start.1 = (bf16[2,1,1024,6,128]{2,4,3,0,1:T(8,128)(2,1)S(1)}, bf16[2,1,1024,6,128]{2,4,3,0,1:T(8,128)(2,1)}, u32[]{:S(2)}, u32[]{:S(2)}) collective-permute-start(bf16[2,1,1024,6,128]{2,4,3,0,1:T(8,128)(2,1)S(1)} %maximum_bitcast_fusion), channel_id=1, source_target_pairs={{8,0},{16,8},{24,16},{32,24},{40,32},{48,40},{56,48},{64,56},{72,6... | collective-permute-start | bytes 9437192 | tf_op jit(solution)/shard_map/ppermute | solution.py:22
  83.7 8.9 %all-to-all-start.1 = ((s32[1,8,6]{2,0,1:T(1,128)}), s32[1,8,6]{2,0,1:T(1,128)S(1)}, u32[]{:S(2)}, u32[]{:S(2)}) async-start(s32[1,8,6]{2,0,1:T(1,128)} %bitcast.10), calls=%async_computation.1 | async-start | bytes 8192 | tf_op jit(solution)/shard_map/all_to_all | solution.py:107
  92.5 25.7 %all-to-all-start = ((bf16[128,8,768]{0,2,1:T(8,128)(2,1)}), bf16[128,8,768]{0,2,1:T(8,128)(2,1)}, u32[]{:S(2)}, u32[]{:S(2)}) async-start(bf16[128,8,768]{0,2,1:T(8,128)(2,1)} %bitcast.107), calls=%async_computation | async-start | bytes 3145728 | tf_op jit(solution)/shard_map/all_to_all | solution.py:104
  174.4 6.9 %copy-start.4 = (bf16[6,1024,128]{1,2,0:T(8,128)(2,1)S(1)}, bf16[6,1024,128]{1,2,0:T(8,128)(2,1)}, u32[]{:S(2)}) copy-start(bf16[6,1024,128]{1,2,0:T(8,128)(2,1)} %custom-call) | copy-start | bytes 4718596
  289.8 1.1 copy-start.5
  328.0 3.5 %copy-start.1 = (s32[48,3]{0,1:T(4,128)S(1)}, s32[48,3]{0,1:T(4,128)}, u32[]{:S(2)}) copy-start(s32[48,3]{0,1:T(4,128)} %param.15) | copy-start | bytes 1732
where the time goes:
time: 336 us; the launch traced here: 332 us
  matrix products  87.7 us (26%)
  waiting for transfers between devices  83.9 us (25%)
  local copies, waits for them, and re-layouts  66.4 us (20%)
  starting transfers between devices  33.5 us (10%)
  other arithmetic  33.3 us (10%)
  blocking collectives  26 us (8%)
    dot_general x6, matrix products, attend_head(): lax.dot_general(queries, keys_near, (((1,), (1,)), ((), ())), preferred_e...  65.4 us
    all_to_all x1, blocking collectives, on_device(): lax.all_to_all(result.reshape(frame_tokens, 1, group_heads * HD), 'head',...  26 us
    dot_general x6, matrix products, attend_head(): jnp.dot(weights.astype(jnp.bfloat16), values_near, preferred_element_type...  22.3 us
    all_to_all x1, waiting for transfers between devices, on_device(): lax.all_to_all(query_wide, 'head', split_axis=1, concat_axis=0, tiled=True)  20.6 us
    all_to_all x1, waiting for transfers between devices, on_device(): lax.all_to_all(key_wide, 'head', split_axis=1, concat_axis=0, tiled=True)  19.2 us
    ppermute x1, waiting for transfers between devices, padded(): lax.ppermute(lax.slice_in_dim(block, block.shape[dim] - width, None, axis...  17.8 us
    slice x2, local copies, waits for them, and re-layouts, attend_group(): values_near = rimmed[1].reshape(3 * frame_tokens, head_count, HD)  16.2 us
    unnamed x28, local copies, waits for them, and re-layouts  16 us
  transfers between devices with their start and end apart: 8, of which 8 were waited for; matrix products, arithmetic and copies ran while one was open for 8% of the time, Pallas kernels for 0%

commit v1 on v0

v1 whole, which is shorter than its diff:
```python
import functools
import math

import jax
import jax.numpy as jnp
import numpy as np
from jax import lax
from jax.experimental import pallas as pl
from jax.experimental.pallas import tpu as pltpu
from jax.sharding import PartitionSpec as P

H = 48
HD = 128
TILE = 128
HT = 4
WT = 2
TILES = HT * WT
SLOTS = H // TILES
FRAMES = 3
NEG = -1e30
LOG2_SCALE = math.log2(math.e) / math.sqrt(HD)
MESH = pl.DeviceIdType.MESH
HALO_CHOICES = (3, 4, 6)


def power(exponent):
    return jnp.where(exponent > 0, 2.0, jnp.where(exponent < 0, 0.5, 1.0)).astype(jnp.float32)


def bytes_of(ref, sem):
    return pltpu.make_async_copy(ref, ref, sem)


def attend(q_ref, kv_ref, score_refs, write, table, slot, first_frame):
    frames = kv_ref.shape[0]

    def biases(row):
        rows = [table[slot, row * HT + r] for r in range(HT)]
        columns = [table[slot, HT * HT + c] for c in range(WT)]
        beside = [table[slot, HT * HT + WT + first_frame + f] for f in range(frames)]
        return lambda f, t, u: rows[t // WT] + columns[abs(t % WT - u)] + beside[f]

    def score(row, s_ref):
        bias = biases(row)
        queries = q_ref[pl.ds(row * WT, WT)].reshape(WT * TILE, HD)
        peak = [None] * WT
        for f in range(frames):
            for t in range(0, TILES, WT):
                keys = kv_ref[f, t : t + WT, 0].reshape(WT * TILE, HD)
                s = lax.dot_general(
                    keys, queries, (((1,), (1,)), ((), ())), preferred_element_type=jnp.float32
                )
                base = (f * TILES + t) * TILE
                s_ref[base : base + WT * TILE, :] = s
                for j in range(WT):
                    for u in range(WT):
                        block = s[j * TILE : (j + 1) * TILE, u * TILE : (u + 1) * TILE]
                        top = jnp.max(block.reshape(TILE // 8, 8, TILE), axis=0) + bias(f, t + j, u)
                        peak[u] = top if peak[u] is None else jnp.maximum(peak[u], top)
        return [jnp.max(p, axis=0, keepdims=True) * LOG2_SCALE for p in peak]

    def combine(row, s_ref, peak):
        bias = biases(row)
        ones = jnp.ones((16, WT * TILE), jnp.bfloat16)
        total = None
        for f in range(frames):
            for t in range(0, TILES, WT):
                base = (f * TILES + t) * TILE
                columns = []
                for u in range(WT):
                    parts = []
                    for j in range(WT):
                        s = s_ref[base + j * TILE : base + (j + 1) * TILE, u * TILE : (u + 1) * TILE]
                        shift = bias(f, t + j, u) - peak[u]
                        parts.append(jnp.exp2(s * LOG2_SCALE + shift).astype(jnp.bfloat16))
                    columns.append(jnp.concatenate(parts, axis=0))
                weights = jnp.concatenate(columns, axis=1)
                values = jnp.concatenate([kv_ref[f, t + j, 1] for j in range(WT)], axis=1)
                values = jnp.concatenate([values, ones], axis=0)
                part = jnp.dot(values, weights, preferred_element_type=jnp.float32)
                total = part if total is None else total + part
        out = total[:HD] * (1.0 / total[HD : HD + 1])
        for u in range(WT):
            write(row * WT + u, out[:, u * TILE : (u + 1) * TILE].T.astype(jnp.bfloat16))

    def rows(i, carry):
        at = [i * 2 + j for j in range(2)]
        peaks = [score(r, s_ref) for r, s_ref in zip(at, score_refs)]
        for r, s_ref, peak in zip(at, score_refs, peaks):
            combine(r, s_ref, peak)
        return carry

    lax.fori_loop(0, HT // 2, rows, 0)


def exchange_kernel(
    halo, frame_total,
    table, kv_stage, q_stage,
    out,
    kv_wide, kv_near, q_near, o_stage, scores_a, scores_b,
    kv_send, kv_recv, q_send, q_recv, halo_send, halo_recv, o_send, o_recv, own_sem,
):
    me = lax.axis_index("head")
    seq = lax.axis_index("seq")
    later = lax.rem(seq + 1, frame_total)
    earlier = lax.rem(seq + frame_total - 1, frame_total)

    def peer(d):
        return lax.rem(me + d, TILES)

    barrier = pltpu.get_barrier_semaphore()
    for d in range(1, TILES):
        pl.semaphore_signal(barrier, inc=1, device_id=(seq, peer(d)), device_id_type=MESH)
    for frame in (later, earlier):
        pl.semaphore_signal(barrier, inc=1, device_id=(frame, me), device_id_type=MESH)
    pl.semaphore_wait(barrier, TILES - 1 + 2)

    def send_kv(s, tile_at):
        for d in range(1, TILES):
            group = peer(d)
            pltpu.make_async_remote_copy(
                src_ref=kv_stage.at[s, group],
                dst_ref=tile_at(s, me),
                send_sem=kv_send.at[s],
                recv_sem=kv_recv.at[s],
                device_id=(seq, group),
                device_id_type=MESH,
            ).start()
        pltpu.make_async_copy(kv_stage.at[s, me], tile_at(s, me), own_sem.at[0, s]).start()

    def send_q(s):
        for d in range(1, TILES):
            group = peer(d)
            pltpu.make_async_remote_copy(
                src_ref=q_stage.at[s, group],
                dst_ref=q_near.at[s, me],
                send_sem=q_send.at[s],
                recv_sem=q_recv.at[s],
                device_id=(seq, group),
                device_id_type=MESH,
            ).start()
        pltpu.make_async_copy(q_stage.at[s, me], q_near.at[s, me], own_sem.at[1, s]).start()

    def wide_tile(s, t):
        return kv_wide.at[s, 1, t]

    def near_tile(s, t):
        return kv_near.at[s - halo, 0, t]

    def halo_copies(s):
        return [
            pltpu.make_async_remote_copy(
                src_ref=kv_wide.at[s, 1],
                dst_ref=kv_wide.at[s, 2 * side],
                send_sem=halo_send.at[s, side],
                recv_sem=halo_recv.at[s, side],
                device_id=(frame, me),
                device_id_type=MESH,
            )
            for side, frame in enumerate((later, earlier))
        ]

    def start_wide_kv(s, carry):
        send_kv(s, wide_tile)
        return carry

    def start_near_kv(s, carry):
        send_kv(s, near_tile)
        return carry

    def start_q(s, carry):
        send_q(s)
        return carry

    def forward(s, carry):
        bytes_of(kv_wide.at[s, 1, pl.ds(0, TILES - 1)], kv_recv.at[s]).wait()
        pltpu.make_async_copy(kv_stage.at[s, me], wide_tile(s, me), own_sem.at[0, s]).wait()
        for copy in halo_copies(s):
            copy.start()
        return carry

    lax.fori_loop(0, halo, start_wide_kv, 0)
    lax.fori_loop(0, halo, start_q, 0)
    if halo < SLOTS:
        lax.fori_loop(halo, SLOTS, start_near_kv, 0)
        lax.fori_loop(halo, SLOTS, start_q, 0)
    lax.fori_loop(0, halo, forward, 0)

    def attend_slot(s, kv_ref, first_frame):
        bytes_of(q_near.at[s, pl.ds(0, TILES - 1)], q_recv.at[s]).wait()
        pltpu.make_async_copy(q_stage.at[s, me], q_near.at[s, me], own_sem.at[1, s]).wait()

        def write(t, tile):
            o_stage[s, t] = tile

        attend(q_near.at[s], kv_ref, (scores_a, scores_b), write, table, s, first_frame)
        for d in range(1, TILES):
            group = peer(d)
            pltpu.make_async_remote_copy(
                src_ref=o_stage.at[s, group],
                dst_ref=out.at[s, me],
                send_sem=o_send.at[s],
                recv_sem=o_recv.at[s],
                device_id=(seq, group),
                device_id_type=MESH,
            ).start()
        pltpu.make_async_copy(o_stage.at[s, me], out.at[s, me], own_sem.at[2, s]).start()

    def wide_slot(s, carry):
        for copy in halo_copies(s):
            copy.wait_recv()
        attend_slot(s, kv_wide.at[s], 0)
        return carry

    def near_slot(s, carry):
        bytes_of(kv_near.at[s - halo, 0, pl.ds(0, TILES - 1)], kv_recv.at[s]).wait()
        pltpu.make_async_copy(kv_stage.at[s, me], near_tile(s, me), own_sem.at[0, s]).wait()
        attend_slot(s, kv_near.at[s - halo], 1)
        return carry

    lax.fori_loop(0, halo, wide_slot, 0)
    if halo < SLOTS:
        lax.fori_loop(halo, SLOTS, near_slot, 0)

    def finish(s, carry):
        bytes_of(kv_stage.at[s, pl.ds(0, TILES - 1)], kv_send.at[s]).wait()
        bytes_of(q_stage.at[s, pl.ds(0, TILES - 1)], q_send.at[s]).wait()
        pltpu.make_async_copy(o_stage.at[s, me], out.at[s, me], own_sem.at[2, s]).wait()
        bytes_of(o_stage.at[s, pl.ds(0, TILES - 1)], o_send.at[s]).wait()
        bytes_of(out.at[s, pl.ds(0, TILES - 1)], o_recv.at[s]).wait()
        return carry

    def finish_halo(s, carry):
        for copy in halo_copies(s):
            copy.wait_send()
        return carry

    lax.fori_loop(0, halo, finish_halo, 0)
    lax.fori_loop(0, SLOTS, finish, 0)


def prepare_kernel(order, q_exp, k_exp, v_exp, q_data, k_data, v_data, kv_out, q_out):
    slot = pl.program_id(0)
    for group in range(TILES):
        head = order[slot * TILES + group]
        columns = pl.ds(pl.multiple_of(head * HD, HD), HD)

        def scaled(ref, exps):
            return (ref[:, columns].astype(jnp.float32) * power(exps[0, head])).astype(jnp.bfloat16)

        kv_out[0, group, 0] = scaled(k_data, k_exp)
        kv_out[0, group, 1] = scaled(v_data, v_exp).T
        q_out[0, group] = scaled(q_data, q_exp)


def prepare(order, q_exp, k_exp, v_exp, q_data, k_data, v_data):
    smem = pl.BlockSpec(memory_space=pltpu.SMEM)
    whole = pl.BlockSpec((TILE, H * HD), lambda i: (0, 0))
    return pl.pallas_call(
        prepare_kernel,
        out_shape=(
            jax.ShapeDtypeStruct((SLOTS, TILES, 2, TILE, HD), jnp.bfloat16),
            jax.ShapeDtypeStruct((SLOTS, TILES, TILE, HD), jnp.bfloat16),
        ),
        grid=(SLOTS,),
        in_specs=[smem] * 4 + [whole] * 3,
        out_specs=(
            pl.BlockSpec((1, TILES, 2, TILE, HD), lambda i: (i, 0, 0, 0, 0)),
            pl.BlockSpec((1, TILES, TILE, HD), lambda i: (i, 0, 0, 0)),
        ),
        compiler_params=pltpu.CompilerParams(vmem_limit_bytes=32 << 20),
        name="prepare",
    )(order, q_exp, k_exp, v_exp, q_data, k_data, v_data)


def exchange(halo, collective_id, frame_total, operands):
    near = max(SLOTS - halo, 1)
    smem = pl.BlockSpec(memory_space=pltpu.SMEM)
    hbm = pl.BlockSpec(memory_space=pl.ANY)
    bf16 = jnp.bfloat16
    tile = (TILE, HD)
    return pl.pallas_call(
        functools.partial(exchange_kernel, halo, frame_total),
        out_shape=jax.ShapeDtypeStruct((SLOTS, TILES) + tile, bf16),
        in_specs=[smem] + [hbm] * 2,
        out_specs=hbm,
        scratch_shapes=[
            pltpu.VMEM((halo, FRAMES, TILES, 2) + tile, bf16),
            pltpu.VMEM((near, 1, TILES, 2) + tile, bf16),
            pltpu.VMEM((SLOTS, TILES) + tile, bf16),
            pltpu.VMEM((SLOTS, TILES) + tile, bf16),
            pltpu.VMEM((FRAMES * TILES * TILE, WT * TILE), jnp.float32),
            pltpu.VMEM((FRAMES * TILES * TILE, WT * TILE), jnp.float32),
            pltpu.SemaphoreType.DMA((SLOTS,)),
            pltpu.SemaphoreType.DMA((SLOTS,)),
            pltpu.SemaphoreType.DMA((SLOTS,)),
            pltpu.SemaphoreType.DMA((SLOTS,)),
            pltpu.SemaphoreType.DMA((halo, 2)),
            pltpu.SemaphoreType.DMA((halo, 2)),
            pltpu.SemaphoreType.DMA((SLOTS,)),
            pltpu.SemaphoreType.DMA((SLOTS,)),
            pltpu.SemaphoreType.DMA((3, SLOTS)),
        ],
        compiler_params=pltpu.CompilerParams(
            collective_id=collective_id, has_side_effects=True, vmem_limit_bytes=50 << 20
        ),
        name=f"exchange_{halo}",
    )(*operands)


def restore_kernel(place, tiles, out):
    heads = out.shape[1] // HD
    for i in range(heads):
        out[:, i * HD : (i + 1) * HD] = tiles[place[pl.program_id(0) * heads + i]]


def restore(place, tiles):
    blocks = 4
    return pl.pallas_call(
        restore_kernel,
        out_shape=jax.ShapeDtypeStruct((TILE, H * HD), jnp.bfloat16),
        grid=(blocks,),
        in_specs=[
            pl.BlockSpec(memory_space=pltpu.SMEM),
            pl.BlockSpec((H, TILE, HD), lambda i: (0, 0, 0)),
        ],
        out_specs=pl.BlockSpec((TILE, H * HD // blocks), lambda i: (0, i)),
        compiler_params=pltpu.CompilerParams(vmem_limit_bytes=16 << 20),
        name="restore",
    )(place, tiles)


def on_device(frame_total, q_data, k_data, v_data, q_exp, k_exp, v_exp, extents):
    index = jnp.arange(H, dtype=jnp.int32)
    sort_key = (1 - extents[:, 0]) * H + index
    place = jnp.sum((sort_key[None, :] < sort_key[:, None]).astype(jnp.int32), axis=1)
    order = jnp.sum(jnp.where(place[None, :] == index[:, None], index[None, :], 0), axis=1)
    reaching = jnp.sum((extents[:, 0] > 0).astype(jnp.int32))
    choice = sum((reaching > n * TILES).astype(jnp.int32) for n in HALO_CHOICES[:-1])
    own = place[None, :] == jnp.arange(SLOTS)[:, None] * TILES + lax.axis_index("head")
    extent = jnp.sum(jnp.where(own[:, :, None], extents[None], 0), axis=1)
    seq = lax.axis_index("seq")
    row = np.arange(HT)
    need = jnp.concatenate(
        [
            jnp.broadcast_to(extent[:, 1:2], (SLOTS, HT * HT)),
            jnp.broadcast_to(extent[:, 2:3], (SLOTS, WT)),
            jnp.broadcast_to(extent[:, 0:1], (SLOTS, FRAMES)),
        ],
        axis=1,
    )
    apart = np.concatenate(
        [np.abs(row[:, None] - row[None]).ravel(), np.arange(WT), np.abs(np.arange(FRAMES) - 1)]
    )
    step = np.concatenate([np.zeros(HT * HT + WT, int), np.arange(FRAMES) - 1])
    inside = (seq + step >= 0) & (seq + step < frame_total)
    table = jnp.where((need >= apart[None]) & inside[None], 0.0, NEG).astype(jnp.float32)
    kv_stage, q_stage = prepare(order, q_exp, k_exp, v_exp, q_data, k_data, v_data)
    operands = (table, kv_stage, q_stage)
    branches = [
        functools.partial(lambda n, i, *ops: exchange(n, i, frame_total, ops), n, i)
        for i, n in enumerate(HALO_CHOICES)
    ]
    tiles = lax.switch(choice, branches, *operands)
    return restore(place, tiles.reshape(H, TILE, HD))


def solution(mesh):
    rows = P(("seq", "head"), None)
    return jax.shard_map(
        functools.partial(on_device, mesh.shape["seq"]),
        mesh=mesh,
        in_specs=(rows,) * 6 + (P(),),
        out_specs=rows,
        check_vma=False,
    )
```

time: 336 us -> 97.9 us (0.29); the launches traced: 332 us -> 97.6 us
  matrix products: 87.7 us -> 0 us
  Pallas kernels: 0 us -> 85.8 us
  waiting for transfers between devices: 83.9 us -> 0 us
  local copies, waits for them, and re-layouts: 66.4 us -> 6.41 us
  starting transfers between devices: 33.5 us -> 0 us
  other arithmetic: 33.3 us -> 3.95 us
  blocking collectives: 26 us -> 0 us
    dot_general x12 -> x0, matrix products: 87.7 us -> none  [the longest x6 65.4 us: attend_head(): lax.dot_general(queries, keys_near, (((1,), (1,)), ((), ())), preferred_e...]
    pallas_call x0 -> x3, Pallas kernels: none -> 85.8 us  [the longest x1 81.2 us: exchange(): pl.pallas_call(functools.partial(exchange_kernel, halo, frame_total), out...]
    all_to_all x6 -> x0, waiting for transfers between devices: 60.6 us -> none  [the longest x1 20.6 us: on_device(): lax.all_to_all(query_wide, 'head', split_axis=1, concat_axis=0, tiled=True)]
    all_to_all x6 -> x0, starting transfers between devices: 28 us -> none  [the longest x1 6.45 us: on_device(): lax.all_to_all(value_scale, 'head', split_axis=1, concat_axis=0, tiled=True)]
    slice x9 -> x0, local copies, waits for them, and re-layouts: 26.3 us -> none  [the longest x2 16.2 us: attend_group(): values_near = rimmed[1].reshape(3 * frame_tokens, head_count, HD)]
    all_to_all x1 -> x0, blocking collectives: 26 us -> none  [on_device(): lax.all_to_all(result.reshape(frame_tokens, 1, group_heads * HD), 'head',...]
    ppermute x2 -> x0, waiting for transfers between devices: 23.3 us -> none  [the longest x1 17.8 us: padded(): lax.ppermute(lax.slice_in_dim(block, block.shape[dim] - width, None, axis...]
    unnamed x28 -> x14, local copies, waits for them, and re-layouts: 16 us -> 6.2 us
  transfers between devices with their start and end apart: 8 -> 0, of which waited for: 8 -> 0; matrix products, arithmetic and copies ran while one was open for 8% -> 0% of each run, Pallas kernels for 0% -> 0%
where the time goes in v1:
time: 97.9 us; the launch traced here: 97.6 us
  Pallas kernels  85.8 us (88%)
  local copies, waits for them, and re-layouts  6.41 us (7%)
  other arithmetic  3.95 us (4%)
  between operations  1.35 us (1%)
    pallas_call x1, Pallas kernels, exchange(): pl.pallas_call(functools.partial(exchange_kernel, halo, frame_total), out...  81.2 us
    unnamed x14, local copies, waits for them, and re-layouts  6.2 us
    pallas_call x1, Pallas kernels, restore(): pl.pallas_call(restore_kernel, out_shape=jax.ShapeDtypeStruct((TILE, H *...  2.35 us
    pallas_call x1, Pallas kernels, prepare(): pl.pallas_call(prepare_kernel, out_shape=(jax.ShapeDtypeStruct((SLOTS, TI...  2.27 us

profile of v1, /device:TPU:1, one launch (start us, length us, event | category | flops | bytes accessed | tf_op | source)
XLA Modules:
  0.0 97.6 jit_solution(1622277564148467863)
XLA Ops:
  0.0 0.7 broadcast_add_fusion
  0.7 0.7 bitcast_add_fusion
  1.3 1.3 %fusion = (s32[]{:T(128)}, s32[48]{0:T(128)S(1)}) fusion(s32[48,3]{0,1:T(4,128)} %param.18), kind=kLoop, calls=%fused_computation.13 | loop fusion | flops 287 | bytes 388 | tf_op jit(solution)/shard_map/reduce_sum | solution.py:338
  4.0 0.2 convert_reduce_fusion.place
  4.1 0.1 select_reduce_fusion.order
  4.3 0.1 broadcast_compare_fusion
  4.3 0.8 select_reduce_fusion.1
  5.2 0.1 broadcast_in_dim.95
  5.3 0.1 broadcast_in_dim.99
  5.3 0.1 broadcast_in_dim.97
  5.4 0.1 pad_add_fusion
  5.5 0.0 copy-start
  5.5 1.4 %copy-done = bf16[128,6144]{1,0:T(8,128)(2,1)S(1)} copy-done((bf16[128,6144]{1,0:T(8,128)(2,1)S(1)}, bf16[128,6144]{1,0:T(8,128)(2,1)}, u32[]{:S(2)}) %copy-start) | copy-done | bytes 1572888
  6.9 0.0 copy-start.1
  6.9 1.4 %copy-done.1 = bf16[128,6144]{1,0:T(8,128)(2,1)S(1)} copy-done((bf16[128,6144]{1,0:T(8,128)(2,1)S(1)}, bf16[128,6144]{1,0:T(8,128)(2,1)}, u32[]{:S(2)}) %copy-start.1) | copy-done | bytes 1572888
  8.3 0.0 copy-start.2
  8.3 1.4 %copy-done.2 = bf16[128,6144]{1,0:T(8,128)(2,1)S(1)} copy-done((bf16[128,6144]{1,0:T(8,128)(2,1)S(1)}, bf16[128,6144]{1,0:T(8,128)(2,1)}, u32[]{:S(2)}) %copy-start.2) | copy-done | bytes 1572888
  9.7 0.0 copy-start.3
  9.7 0.7 copy-done.3
  10.4 0.0 copy-start.4
  10.4 0.7 copy-done.4
  11.0 0.0 copy-start.5
  11.0 0.7 copy-done.5
  11.7 0.0 copy-start.6
  11.7 2.3 %prepare.1 = (bf16[6,8,2,128,128]{4,3,2,1,0:T(8,128)(2,1)S(1)}, bf16[6,8,128,128]{3,2,1,0:T(8,128)(2,1)S(1)}) custom-call(s32[48]{0:T(128)S(1)} %select_reduce_fusion.order, s32[1,48]{1,0:T(1,128)S(1)} %copy-done.3, s32[1,48]{1,0:T(1,128)S(1)} %copy-done.4, s32[1,48]{1,0:T(1,128)S(1)} %copy-done.5, bf16[128,6144]{1,0:T(8,128)(2,1)S(1)} %copy-done, ...), custom_call_target="tpu_custom_call" | custom-call | tf_op jit(solution)/shard_map/prepare/pallas_call | solution.py:259
  14.0 0.0 copy-done.6
  14.0 81.3 %conditional.1 = (bf16[48,128,128]{2,1,0:T(8,128)(2,1)S(1)}) conditional(s32[]{:T(128)} %clamp.3, (s32[1,21]{1,0:T(1,128)S(1)}, s32[6,21]{1,0:T(8,128)S(1)}, s32[21]{0:T(128)S(1)}, bf16[6,8,2,128,128]{4,3,2,1,0:T(8,128)(2,1)S(1)}, bf16[6,8,128,128]{3,2,1,0:T(8,128)(2,1)S(1)}) %tuple.77, (s32[1,21]{1,0:T(1,128)S(1)}, ...), branch_computations={%region_4.5_spmd, %region_5.6_spmd, %region_6.7_spmd} | conditional | flops 441 | bytes 1226 | solution.py:364
  14.0 81.2 %exchange_3.2 = bf16[6,8,128,128]{3,2,1,0:T(8,128)(2,1)S(1)} custom-call(f32[6,21]{1,0:T(8,128)S(1)} %and_select_fusion.table, bf16[6,8,2,128,128]{4,3,2,1,0:T(8,128)(2,1)S(1)} %get-tuple-element.139.kv_stage, bf16[6,8,128,128]{3,2,1,0:T(8,128)(2,1)S(1)} %get-tuple-element.140.q_stage), custom_call_target="tpu_custom_call" | custom-call | tf_op jit(solution)/shard_map/cond/branch_0_fun/exchange_3/pallas_call | solution.py:282
  95.2 2.3 %restore.1 = bf16[128,6144]{1,0:T(8,128)(2,1)} custom-call(s32[48]{0:T(128)S(1)} %convert_reduce_fusion.place, bf16[48,128,128]{2,1,0:T(8,128)(2,1)S(1)} %get-tuple-element.160.tiles), custom_call_target="tpu_custom_call" | custom-call | tf_op jit(solution)/shard_map/restore/pallas_call | solution.py:319
  (4 shorter events, 0.0 us)
Async XLA Ops:
  5.5 1.4 %copy-start = (bf16[128,6144]{1,0:T(8,128)(2,1)S(1)}, bf16[128,6144]{1,0:T(8,128)(2,1)}, u32[]{:S(2)}) copy-start(bf16[128,6144]{1,0:T(8,128)(2,1)} %q_data.1) | copy-start | bytes 4718596
  6.9 1.4 %copy-start.1 = (bf16[128,6144]{1,0:T(8,128)(2,1)S(1)}, bf16[128,6144]{1,0:T(8,128)(2,1)}, u32[]{:S(2)}) copy-start(bf16[128,6144]{1,0:T(8,128)(2,1)} %k_data.1) | copy-start | bytes 4718596
  8.3 1.4 %copy-start.2 = (bf16[128,6144]{1,0:T(8,128)(2,1)S(1)}, bf16[128,6144]{1,0:T(8,128)(2,1)}, u32[]{:S(2)}) copy-start(bf16[128,6144]{1,0:T(8,128)(2,1)} %v_data.1) | copy-start | bytes 4718596
  9.7 0.7 copy-start.3
  10.4 0.7 copy-start.4
  11.0 0.7 copy-start.5
  11.7 2.3 %copy-start.6 = (s32[1,21]{1,0:T(1,128)S(1)}, s32[1,21]{1,0:T(1,128)}, u32[]{:S(2)}) copy-start(s32[1,21]{1,0:T(1,128)} %constant.57.clone) | copy-start | bytes 256

commit v2 on v1

--- a/solution.py
+++ b/solution.py
@@ -3,7 +3,6 @@
 
 import jax
 import jax.numpy as jnp
-import numpy as np
 from jax import lax
 from jax.experimental import pallas as pl
 from jax.experimental.pallas import tpu as pltpu
@@ -20,7 +19,8 @@
 NEG = -1e30
 LOG2_SCALE = math.log2(math.e) / math.sqrt(HD)
 MESH = pl.DeviceIdType.MESH
-HALO_CHOICES = (3, 4, 6)
+PLANS = ((5, 2), (5, 3), (5, 5), (6, 4), (6, 6))
+TABLE = (SLOTS + TILES, HT * HT + WT + FRAMES)
 
 
 def power(exponent):
@@ -29,6 +29,10 @@
 
 def bytes_of(ref, sem):
     return pltpu.make_async_copy(ref, ref, sem)
+
+
+def block_max(s):
+    return jnp.max(s.reshape(s.shape[0] // 8, 8, s.shape[1]), axis=0)
 
 
 def attend(q_ref, kv_ref, score_refs, write, table, slot, first_frame):
@@ -55,7 +59,7 @@
                 for j in range(WT):
                     for u in range(WT):
                         block = s[j * TILE : (j + 1) * TILE, u * TILE : (u + 1) * TILE]
-                        top = jnp.max(block.reshape(TILE // 8, 8, TILE), axis=0) + bias(f, t + j, u)
+                        top = block_max(block) + bias(f, t + j, u)
                         peak[u] = top if peak[u] is None else jnp.maximum(peak[u], top)
         return [jnp.max(p, axis=0, keepdims=True) * LOG2_SCALE for p in peak]
 
@@ -93,13 +97,50 @@
     lax.fori_loop(0, HT // 2, rows, 0)
 
 
+def attend_row(queries, kv_ref, head, table):
+    frames = kv_ref.shape[0]
+    row = SLOTS + head
+    columns = [table[row, c] for c in range(WT)]
+    beside = [table[row, WT + f] for f in range(frames)]
+    scores = []
+    peak = None
+    for f in range(frames):
+        for c in range(WT):
+            keys = kv_ref[f, c, head, 0]
+            s = lax.dot_general(
+                keys, queries, (((1,), (1,)), ((), ())), preferred_element_type=jnp.float32
+            )
+            scores.append(s)
+            top = block_max(s) + (columns[c] + beside[f])
+            peak = top if peak is None else jnp.maximum(peak, top)
+    peak = jnp.max(peak, axis=0, keepdims=True) * LOG2_SCALE
+    ones = jnp.ones((16, WT * TILE), jnp.bfloat16)
+    total = None
+    for f in range(frames):
+        weights = jnp.concatenate(
+            [
+                jnp.exp2(scores[f * WT + c] * LOG2_SCALE + (columns[c] + beside[f] - peak))
+                for c in range(WT)
+            ],
+            axis=0,
+        ).astype(jnp.bfloat16)
+        values = jnp.concatenate([kv_ref[f, c, head, 1] for c in range(WT)], axis=1)
+        values = jnp.concatenate([values, ones], axis=0)
+        part = jnp.dot(values, weights, preferred_element_type=jnp.float32)
+        total = part if total is None else total + part
+    return (total[:HD] * (1.0 / total[HD : HD + 1])).T.astype(jnp.bfloat16)
+
+
 def exchange_kernel(
-    halo, frame_total,
+    slots, halo, frame_total,
     table, kv_stage, q_stage,
     out,
-    kv_wide, kv_near, q_near, o_stage, scores_a, scores_b,
+    kv_wide, kv_near, kv_row, q_near, o_stage, scores_a, scores_b,
     kv_send, kv_recv, q_send, q_recv, halo_send, halo_recv, o_send, o_recv, own_sem,
+    row_send, row_recv, side_send, side_recv,
 ):
+    by_row = slots < SLOTS
+    last = SLOTS - 1
     me = lax.axis_index("head")
     seq = lax.axis_index("seq")
     later = lax.rem(seq + 1, frame_total)
@@ -160,12 +201,45 @@
             for side, frame in enumerate((later, earlier))
         ]
 
+    column = lax.rem(me, WT)
+    sibling = me + 1 - 2 * column
+
+    def to_sibling(source, f):
+        return pltpu.make_async_remote_copy(
+            src_ref=source,
+            dst_ref=kv_row.at[f, column],
+            send_sem=side_send.at[f],
+            recv_sem=side_recv.at[f],
+            device_id=(seq, sibling),
+            device_id_type=MESH,
+        )
+
+    def row_halo():
+        return [
+            pltpu.make_async_remote_copy(
+                src_ref=kv_stage.at[last],
+                dst_ref=kv_row.at[2 * side, column],
+                send_sem=row_send.at[side],
+                recv_sem=row_recv.at[side],
+                device_id=(frame, me),
+                device_id_type=MESH,
+            )
+            for side, frame in enumerate((later, earlier))
+        ]
+
+    def own_row():
+        return [
+            pltpu.make_async_copy(kv_stage.at[last], kv_row.at[1, column], own_sem.at[0, last]),
+            pltpu.make_async_copy(q_stage.at[last], q_near.at[last], own_sem.at[1, last]),
+        ]
+
     def start_wide_kv(s, carry):
         send_kv(s, wide_tile)
         return carry
 
     def start_near_kv(s, carry):
         send_kv(s, near_tile)
+        send_q(s)
         return carry
 
     def start_q(s, carry):
@@ -179,12 +253,39 @@
             copy.start()
         return carry
 
-    lax.fori_loop(0, halo, start_wide_kv, 0)
+    send_kv(0, wide_tile)
+    if by_row:
+        for copy in row_halo():
+            copy.start()
+        to_sibling(kv_stage.at[last], 1).start()
+        for copy in own_row():
+            copy.start()
+    lax.fori_loop(1, halo, start_wide_kv, 0)
     lax.fori_loop(0, halo, start_q, 0)
-    if halo < SLOTS:
-        lax.fori_loop(halo, SLOTS, start_near_kv, 0)
-        lax.fori_loop(halo, SLOTS, start_q, 0)
-    lax.fori_loop(0, halo, forward, 0)
+    if halo < slots:
+        lax.fori_loop(halo, slots, start_near_kv, 0)
+    lax.fori_loop(0, 2, forward, 0)
+    if by_row:
+        for side, copy in enumerate(row_halo()):
+            copy.wait_recv()
+            to_sibling(kv_row.at[2 * side, column], 2 * side).start()
+    if halo > 2:
+        lax.fori_loop(2, halo, forward, 0)
+
+    if by_row:
+        for copy in own_row():
+            copy.wait()
+        for f, source in enumerate((kv_row.at[0, column], kv_stage.at[last], kv_row.at[2, column])):
+            to_sibling(source, f).wait_recv()
+
+        def row_heads(i, carry):
+            for j in range(2):
+                head = i * 2 + j
+                o_stage[last, head] = attend_row(q_near[last, head], kv_row, head, table)
+            return carry
+
+        lax.fori_loop(0, TILES // 2, row_heads, 0)
+        pltpu.make_async_copy(o_stage.at[last], out.at[last], own_sem.at[2, last]).start()
 
     def attend_slot(s, kv_ref, first_frame):
         bytes_of(q_near.at[s, pl.ds(0, TILES - 1)], q_recv.at[s]).wait()
@@ -218,9 +319,20 @@
         attend_slot(s, kv_near.at[s - halo], 1)
         return carry
 
-    lax.fori_loop(0, halo, wide_slot, 0)
-    if halo < SLOTS:
-        lax.fori_loop(halo, SLOTS, near_slot, 0)
+    near = slots - halo
+    first = max(halo - near, 0)
+
+    def pair(j, carry):
+        near_slot(halo + j, 0)
+        wide_slot(first + j, 0)
+        return carry
+
+    if first:
+        lax.fori_loop(0, first, wide_slot, 0)
+    if near:
+        lax.fori_loop(0, min(near, halo), pair, 0)
+    if near > halo:
+        lax.fori_loop(halo + halo, slots, near_slot, 0)
 
     def finish(s, carry):
         bytes_of(kv_stage.at[s, pl.ds(0, TILES - 1)], kv_send.at[s]).wait()
@@ -236,57 +348,170 @@
         return carry
 
     lax.fori_loop(0, halo, finish_halo, 0)
-    lax.fori_loop(0, SLOTS, finish, 0)
-
-
-def prepare_kernel(order, q_exp, k_exp, v_exp, q_data, k_data, v_data, kv_out, q_out):
-    slot = pl.program_id(0)
-    for group in range(TILES):
-        head = order[slot * TILES + group]
+    if by_row:
+        for copy in row_halo():
+            copy.wait_send()
+        for f, source in enumerate((kv_row.at[0, column], kv_stage.at[last], kv_row.at[2, column])):
+            to_sibling(source, f).wait_send()
+        pltpu.make_async_copy(o_stage.at[last], out.at[last], own_sem.at[2, last]).wait()
+    lax.fori_loop(0, slots, finish, 0)
+
+
+def prepare_kernel(
+    frame_total,
+    extents, q_exp, k_exp, v_exp, q_data, k_data, v_data,
+    table, place, plan, kv_out, q_out,
+    order, q_in, k_in, v_in, kv_stage, q_stage, in_sem, out_sem,
+):
+    loads = [
+        pltpu.make_async_copy(src, dst, in_sem.at[i])
+        for i, (src, dst) in enumerate(((k_data, k_in), (v_data, v_in), (q_data, q_in)))
+    ]
+    for load in loads:
+        load.start()
+
+    zero = jnp.int32(0)
+    reach = [(extents[0, h] >= 1).astype(jnp.int32) for h in range(H)]
+    flat = [(extents[1, h] <= 0).astype(jnp.int32) for h in range(H)]
+    reaching = sum(reach, zero)
+    flat_reaching = sum((r * f for r, f in zip(reach, flat)), zero)
+    by_row = (sum(flat, zero) >= TILES).astype(jnp.int32)
+    row_reaching = by_row * jnp.minimum(flat_reaching, TILES)
+    rest_reaching = reaching - row_reaching
+    next_row_reach, next_row_rest = zero, row_reaching
+    next_reach, next_rest = zero, rest_reaching
+    for h in range(H):
+        row_index = jnp.where(reach[h] > 0, next_row_reach, next_row_rest)
+        in_row = by_row * flat[h] * (row_index < TILES).astype(jnp.int32)
+        outside = 1 - in_row
+        spot = jnp.where(
+            in_row > 0,
+            H - TILES + row_index,
+            jnp.where(reach[h] > 0, next_reach, next_rest),
+        )
+        next_row_reach += in_row * reach[h]
+        next_row_rest += in_row * (1 - reach[h])
+        next_reach += outside * reach[h]
+        next_rest += outside * (1 - reach[h])
+        order[spot] = h
+        place[h] = spot
+    wide = [rest_reaching > n * TILES for n in (2, 3, 4)]
+    with_row = wide[0].astype(jnp.int32) + wide[1].astype(jnp.int32)
+    plan[0] = jnp.where(by_row > 0, with_row, 3 + wide[2].astype(jnp.int32))
+
+    me = lax.axis_index("head")
+    seq = lax.axis_index("seq")
+    column = lax.rem(me, WT)
+
+    def within(condition):
+        return jnp.where(condition, 0.0, NEG).astype(jnp.float32)
+
+    def beside(head, f):
+        inside = (seq + f - 1 >= 0) & (seq + f - 1 < frame_total)
+        return within((extents[0, head] >= abs(f - 1)) & inside)
+
+    for s in range(SLOTS):
+        head = order[s * TILES + me]
+        for r in range(HT):
+            for t in range(HT):
+                table[s, r * HT + t] = within(extents[1, head] >= abs(r - t))
+        for c in range(WT):
+            table[s, HT * HT + c] = within(extents[2, head] >= c)
+        for f in range(FRAMES):
+            table[s, HT * HT + WT + f] = beside(head, f)
+    for i in range(TILES):
+        head = order[H - TILES + i]
+        for c in range(WT):
+            table[SLOTS + i, c] = within(extents[2, head] >= jnp.abs(column - c))
+        for f in range(FRAMES):
+            table[SLOTS + i, WT + f] = beside(head, f)
+
+    def scaled(ref, exps, head):
         columns = pl.ds(pl.multiple_of(head * HD, HD), HD)
-
-        def scaled(ref, exps):
-            return (ref[:, columns].astype(jnp.float32) * power(exps[0, head])).astype(jnp.bfloat16)
-
-        kv_out[0, group, 0] = scaled(k_data, k_exp)
-        kv_out[0, group, 1] = scaled(v_data, v_exp).T
-        q_out[0, group] = scaled(q_data, q_exp)
-
-
-def prepare(order, q_exp, k_exp, v_exp, q_data, k_data, v_data):
+        return (ref[:, columns].astype(jnp.float32) * power(exps[0, head])).astype(jnp.bfloat16)
+
+    def kv_copy(s, which):
+        return pltpu.make_async_copy(
+            kv_stage.at[s, :, which], kv_out.at[s, :, which], out_sem.at[which, s]
+        )
+
+    def q_copy(s):
+        return pltpu.make_async_copy(q_stage.at[s], q_out.at[s], out_sem.at[2, s])
+
+    def stage_keys(s, carry):
+        for g in range(TILES):
+            kv_stage[s, g, 0] = scaled(k_in, k_exp, order[s * TILES + g])
+        kv_copy(s, 0).start()
+        return carry
+
+    def stage_values(s, carry):
+        for g in range(TILES):
+            kv_stage[s, g, 1] = scaled(v_in, v_exp, order[s * TILES + g]).T
+        kv_copy(s, 1).start()
+        return carry
+
+    def stage_queries(s, carry):
+        for g in range(TILES):
+            q_stage[s, g] = scaled(q_in, q_exp, order[s * TILES + g])
+        q_copy(s).start()
+        return carry
+
+    for load, stage in zip(loads, (stage_keys, stage_values, stage_queries)):
+        load.wait()
+        lax.fori_loop(0, SLOTS, stage, 0)
+    for s in range(SLOTS):
+        kv_copy(s, 0).wait()
+        kv_copy(s, 1).wait()
+        q_copy(s).wait()
+
+
+def prepare(frame_total, extents, q_exp, k_exp, v_exp, q_data, k_data, v_data):
     smem = pl.BlockSpec(memory_space=pltpu.SMEM)
-    whole = pl.BlockSpec((TILE, H * HD), lambda i: (0, 0))
+    hbm = pl.BlockSpec(memory_space=pl.ANY)
+    bf16 = jnp.bfloat16
+    kv = (SLOTS, TILES, 2, TILE, HD)
+    q = (SLOTS, TILES, TILE, HD)
+    whole = pltpu.VMEM((TILE, H * HD), bf16)
     return pl.pallas_call(
-        prepare_kernel,
+        functools.partial(prepare_kernel, frame_total),
         out_shape=(
-            jax.ShapeDtypeStruct((SLOTS, TILES, 2, TILE, HD), jnp.bfloat16),
-            jax.ShapeDtypeStruct((SLOTS, TILES, TILE, HD), jnp.bfloat16),
+            jax.ShapeDtypeStruct(TABLE, jnp.float32),
+            jax.ShapeDtypeStruct((H,), jnp.int32),
+            jax.ShapeDtypeStruct((1,), jnp.int32),
+            jax.ShapeDtypeStruct(kv, bf16),
+            jax.ShapeDtypeStruct(q, bf16),
         ),
-        grid=(SLOTS,),
-        in_specs=[smem] * 4 + [whole] * 3,
-        out_specs=(
-            pl.BlockSpec((1, TILES, 2, TILE, HD), lambda i: (i, 0, 0, 0, 0)),
-            pl.BlockSpec((1, TILES, TILE, HD), lambda i: (i, 0, 0, 0)),
-        ),
-        compiler_params=pltpu.CompilerParams(vmem_limit_bytes=32 << 20),
+        in_specs=[smem] * 4 + [hbm] * 3,
+        out_specs=(smem, smem, smem, hbm, hbm),
+        scratch_shapes=[
+            pltpu.SMEM((H,), jnp.int32),
+            whole, whole, whole,
+            pltpu.VMEM(kv, bf16),
+            pltpu.VMEM(q, bf16),
+            pltpu.SemaphoreType.DMA((3,)),
+            pltpu.SemaphoreType.DMA((3, SLOTS)),
+        ],
+        compiler_params=pltpu.CompilerParams(vmem_limit_bytes=60 << 20),
         name="prepare",
-    )(order, q_exp, k_exp, v_exp, q_data, k_data, v_data)
-
-
-def exchange(halo, collective_id, frame_total, operands):
-    near = max(SLOTS - halo, 1)
+    )(extents, q_exp, k_exp, v_exp, q_data, k_data, v_data)
+
+
+def exchange(slots, halo, collective_id, frame_total, operands):
+    near = max(slots - halo, 1)
+    rows = TILES if slots < SLOTS else 1
     smem = pl.BlockSpec(memory_space=pltpu.SMEM)
     hbm = pl.BlockSpec(memory_space=pl.ANY)
     bf16 = jnp.bfloat16
     tile = (TILE, HD)
     return pl.pallas_call(
-        functools.partial(exchange_kernel, halo, frame_total),
+        functools.partial(exchange_kernel, slots, halo, frame_total),
         out_shape=jax.ShapeDtypeStruct((SLOTS, TILES) + tile, bf16),
         in_specs=[smem] + [hbm] * 2,
         out_specs=hbm,
         scratch_shapes=[
             pltpu.VMEM((halo, FRAMES, TILES, 2) + tile, bf16),
             pltpu.VMEM((near, 1, TILES, 2) + tile, bf16),
+            pltpu.VMEM((FRAMES, WT, rows, 2) + tile, bf16),
             pltpu.VMEM((SLOTS, TILES) + tile, bf16),
             pltpu.VMEM((SLOTS, TILES) + tile, bf16),
             pltpu.VMEM((FRAMES * TILES * TILE, WT * TILE), jnp.float32),
@@ -300,68 +525,46 @@
             pltpu.SemaphoreType.DMA((SLOTS,)),
             pltpu.SemaphoreType.DMA((SLOTS,)),
             pltpu.SemaphoreType.DMA((3, SLOTS)),
+            pltpu.SemaphoreType.DMA((2,)),
+            pltpu.SemaphoreType.DMA((2,)),
+            pltpu.SemaphoreType.DMA((FRAMES,)),
+            pltpu.SemaphoreType.DMA((FRAMES,)),
         ],
         compiler_params=pltpu.CompilerParams(
-            collective_id=collective_id, has_side_effects=True, vmem_limit_bytes=50 << 20
+            collective_id=collective_id, has_side_effects=True, vmem_limit_bytes=60 << 20
         ),
-        name=f"exchange_{halo}",
+        name=f"exchange_{slots}_{halo}",
     )(*operands)
 
 
-def restore_kernel(place, tiles, out):
-    heads = out.shape[1] // HD
-    for i in range(heads):
-        out[:, i * HD : (i + 1) * HD] = tiles[place[pl.program_id(0) * heads + i]]
+def restore_kernel(place, tiles, out, sem):
+    for h in range(H):
+        pltpu.make_async_copy(tiles.at[place[h]], out.at[:, pl.ds(h * HD, HD)], sem).start()
+    pltpu.make_async_copy(out, out, sem).wait()
 
 
 def restore(place, tiles):
-    blocks = 4
+    hbm = pl.BlockSpec(memory_space=pl.ANY)
     return pl.pallas_call(
         restore_kernel,
         out_shape=jax.ShapeDtypeStruct((TILE, H * HD), jnp.bfloat16),
-        grid=(blocks,),
-        in_specs=[
-            pl.BlockSpec(memory_space=pltpu.SMEM),
-            pl.BlockSpec((H, TILE, HD), lambda i: (0, 0, 0)),
-        ],
-        out_specs=pl.BlockSpec((TILE, H * HD // blocks), lambda i: (0, i)),
-        compiler_params=pltpu.CompilerParams(vmem_limit_bytes=16 << 20),
+        in_specs=[pl.BlockSpec(memory_space=pltpu.SMEM), hbm],
+        out_specs=hbm,
+        scratch_shapes=[pltpu.SemaphoreType.DMA(())],
+        compiler_params=pltpu.CompilerParams(vmem_limit_bytes=60 << 20),
         name="restore",
     )(place, tiles)
 
 
 def on_device(frame_total, q_data, k_data, v_data, q_exp, k_exp, v_exp, extents):
-    index = jnp.arange(H, dtype=jnp.int32)
-    sort_key = (1 - extents[:, 0]) * H + index
-    place = jnp.sum((sort_key[None, :] < sort_key[:, None]).astype(jnp.int32), axis=1)
-    order = jnp.sum(jnp.where(place[None, :] == index[:, None], index[None, :], 0), axis=1)
-    reaching = jnp.sum((extents[:, 0] > 0).astype(jnp.int32))
-    choice = sum((reaching > n * TILES).astype(jnp.int32) for n in HALO_CHOICES[:-1])
-    own = place[None, :] == jnp.arange(SLOTS)[:, None] * TILES + lax.axis_index("head")
-    extent = jnp.sum(jnp.where(own[:, :, None], extents[None], 0), axis=1)
-    seq = lax.axis_index("seq")
-    row = np.arange(HT)
-    need = jnp.concatenate(
-        [
-            jnp.broadcast_to(extent[:, 1:2], (SLOTS, HT * HT)),
-            jnp.broadcast_to(extent[:, 2:3], (SLOTS, WT)),
-            jnp.broadcast_to(extent[:, 0:1], (SLOTS, FRAMES)),
-        ],
-        axis=1,
+    table, place, plan, kv_stage, q_stage = prepare(
+        frame_total, extents.T, q_exp, k_exp, v_exp, q_data, k_data, v_data
     )
-    apart = np.concatenate(
-        [np.abs(row[:, None] - row[None]).ravel(), np.arange(WT), np.abs(np.arange(FRAMES) - 1)]
-    )
-    step = np.concatenate([np.zeros(HT * HT + WT, int), np.arange(FRAMES) - 1])
-    inside = (seq + step >= 0) & (seq + step < frame_total)
-    table = jnp.where((need >= apart[None]) & inside[None], 0.0, NEG).astype(jnp.float32)
-    kv_stage, q_stage = prepare(order, q_exp, k_exp, v_exp, q_data, k_data, v_data)
-    operands = (table, kv_stage, q_stage)
     branches = [
-        functools.partial(lambda n, i, *ops: exchange(n, i, frame_total, ops), n, i)
-        for i, n in enumerate(HALO_CHOICES)
+        functools.partial(lambda p, i, *ops: exchange(*p, i, frame_total, ops), p, i)
+        for i, p in enumerate(PLANS)
     ]
-    tiles = lax.switch(choice, branches, *operands)
+    tiles = lax.switch(plan[0], branches, table, kv_stage, q_stage)
     return restore(place, tiles.reshape(H, TILE, HD))
 
 

time: 97.9 us -> 127 us (1.30)
  Pallas kernels: 85.8 us -> 125 us
  local copies, waits for them, and re-layouts: 6.41 us -> 0 us
  other arithmetic: 3.95 us -> 0 us
    pallas_call x1, Pallas kernels: 2.35 us -> 49.4 us  [restore(): pl.pallas_call(restore_kernel, out_shape=jax.ShapeDtypeStruct((TILE, H *...]
    pallas_call x2, Pallas kernels: 83.5 us -> 76.1 us  [the longest x1 70.3 us: exchange(): pl.pallas_call(functools.partial(exchange_kernel, slots, halo, frame_tota...]
    unnamed x14 -> x0, local copies, waits for them, and re-layouts: 6.2 us -> none
    reduce_sum x4 -> x0, other arithmetic: 2.44 us -> none  [the longest x1 1.32 us: on_device(): reaching = jnp.sum((extents[:, 0] > 0).astype(jnp.int32))]
    add x3 -> x0, other arithmetic: 1.35 us -> none  [the longest x1 0.69 us: on_device(): sort_key = (1 - extents[:, 0]) * H + index]
where the time goes in v2:
time: 127 us
  Pallas kernels  125 us (98%)
    pallas_call x1, Pallas kernels, exchange(): pl.pallas_call(functools.partial(exchange_kernel, slots, halo, frame_tota...  70.3 us
    pallas_call x1, Pallas kernels, restore(): pl.pallas_call(restore_kernel, out_shape=jax.ShapeDtypeStruct((TILE, H *...  49.4 us
    pallas_call x1, Pallas kernels, prepare(): pl.pallas_call(functools.partial(prepare_kernel, frame_total), out_shape=...  5.8 us

profile of v2, /device:TPU:1, one launch (start us, length us, event | category | flops | bytes accessed | tf_op | source)
XLA Modules:
  0.0 126.6 jit_solution(11765844153575975444)
XLA Ops:
  0.0 5.8 %prepare.1 = (f32[14,21]{1,0:T(8,128)S(1)}, s32[48]{0:T(128)}, s32[1]{0:T(128)}, bf16[6,8,2,128,128]{4,3,2,1,0:T(8,128)(2,1)S(1)}, bf16[6,8,128,128]{3,2,1,0:T(8,128)(2,1)}) custom-call(s32[3,48]{1,0:T(4,128)} %bitcast.12, s32[1,48]{1,0:T(1,128)} %q_exp.1, s32[1,48]{1,0:T(1,128)} %k_exp.1, s32[1,48]{1,0:T(1,128)} %v_exp.1, bf16[128,6144]{1,0:T(8,128)(2,1)} %q_data.1, ...), custom_call_target="tpu_custom_call" | custom-call | tf_op jit(solution)/shard_map/prepare/pallas_call | solution.py:475
  6.4 70.5 %conditional.1 = (bf16[48,128,128]{2,1,0:T(8,128)(2,1)}) conditional(s32[]{:T(128)} %bitcast.6, (f32[14,21]{1,0:T(8,128)S(1)}, bf16[6,8,2,128,128]{4,3,2,1,0:T(8,128)(2,1)S(1)}, bf16[6,8,128,128]{3,2,1,0:T(8,128)(2,1)}) %tuple.25, (f32[14,21]{1,0:T(8,128)S(1)}, bf16[6,8,2,128,128]{4,3,2,1,0:T(8,128)(2,1)S(1)}, ...), branch_computations={%region_0.0_spmd, %region_1.0_spmd, %region_2.0_spmd, %region_3.0_... | conditional | bytes 8 | solution.py:567
  6.5 70.3 %exchange_5_3.1 = bf16[6,8,128,128]{3,2,1,0:T(8,128)(2,1)} custom-call(f32[14,21]{1,0:T(8,128)S(1)} %get-tuple-element.45.table, bf16[6,8,2,128,128]{4,3,2,1,0:T(8,128)(2,1)S(1)} %get-tuple-element.46.kv_stage, bf16[6,8,128,128]{3,2,1,0:T(8,128)(2,1)} %get-tuple-element.47.q_stage), custom_call_target="tpu_custom_call" | custom-call | tf_op jit(solution)/shard_map/cond/branch_1_fun/exchange_5_3/pallas_call | solution.py:506
  77.0 49.4 %restore.1 = bf16[128,6144]{1,0:T(8,128)(2,1)} custom-call(s32[48]{0:T(128)} %get-tuple-element.62.place, bf16[48,128,128]{2,1,0:T(8,128)(2,1)} %get-tuple-element.67.tiles), custom_call_target="tpu_custom_call" | custom-call | tf_op jit(solution)/shard_map/restore/pallas_call | solution.py:548

commit v3 on v2

v3 whole, which is shorter than its diff:
```python
import functools
import math

import jax
import jax.numpy as jnp
from jax import lax
from jax.experimental import pallas as pl
from jax.experimental.pallas import tpu as pltpu
from jax.sharding import PartitionSpec as P

H = 48
HD = 128
TILE = 128
HT = 4
WT = 2
TILES = HT * WT
HALF = TILES // 2
FRAMES = 3
NEG = -1e30
LOG2_SCALE = math.log2(math.e) / math.sqrt(HD)
MESH = pl.DeviceIdType.MESH

PLANS = ((9, 3), (10, 3), (12, 6))
ROW_HEADS = 12
ROW_REACH = 8

SLOTS = H // TILES
ENTRIES = HT * HT + WT + FRAMES
ROW_TABLE = SLOTS * ENTRIES
ROW_ENTRIES = WT + FRAMES
TABLE = ROW_TABLE + ROW_HEADS * ROW_ENTRIES


def bytes_of(ref, sem):
    return pltpu.make_async_copy(ref, ref, sem)


def block_max(s):
    return jnp.max(s.reshape(s.shape[0] // 8, 8, s.shape[1]), axis=0)


def attend(q_ref, kv_ref, score_refs, write, table, slot, first_frame):
    frames = kv_ref.shape[0]
    entry = slot * ENTRIES

    def biases(row):
        rows = [table[entry + row * HT + r] for r in range(HT)]
        columns = [table[entry + HT * HT + c] for c in range(WT)]
        beside = [table[entry + HT * HT + WT + first_frame + f] for f in range(frames)]
        return lambda f, t, u: rows[t // WT] + columns[abs(t % WT - u)] + beside[f]

    def score(row, s_ref):
        bias = biases(row)
        queries = q_ref[pl.ds(row * WT, WT)].reshape(WT * TILE, HD)
        peak = [None] * WT
        for f in range(frames):
            for t in range(0, TILES, WT):
                keys = kv_ref[f, t : t + WT, 0].reshape(WT * TILE, HD)
                s = lax.dot_general(
                    keys, queries, (((1,), (1,)), ((), ())), preferred_element_type=jnp.float32
                )
                base = (f * TILES + t) * TILE
                s_ref[base : base + WT * TILE, :] = s
                for j in range(WT):
                    for u in range(WT):
                        block = s[j * TILE : (j + 1) * TILE, u * TILE : (u + 1) * TILE]
                        top = block_max(block) + bias(f, t + j, u)
                        peak[u] = top if peak[u] is None else jnp.maximum(peak[u], top)
        return [jnp.max(p, axis=0, keepdims=True) * LOG2_SCALE for p in peak]

    def combine(row, s_ref, peak):
        bias = biases(row)
        ones = jnp.ones((16, WT * TILE), jnp.bfloat16)
        total = None
        for f in range(frames):
            for t in range(0, TILES, WT):
                base = (f * TILES + t) * TILE
                columns = []
                for u in range(WT):
                    parts = []
                    for j in range(WT):
                        s = s_ref[base + j * TILE : base + (j + 1) * TILE, u * TILE : (u + 1) * TILE]
                        shift = bias(f, t + j, u) - peak[u]
                        parts.append(jnp.exp2(s * LOG2_SCALE + shift).astype(jnp.bfloat16))
                    columns.append(jnp.concatenate(parts, axis=0))
                weights = jnp.concatenate(columns, axis=1)
                values = jnp.concatenate([kv_ref[f, t + j, 1] for j in range(WT)], axis=1)
                values = jnp.concatenate([values, ones], axis=0)
                part = jnp.dot(values, weights, preferred_element_type=jnp.float32)
                total = part if total is None else total + part
        out = total[:HD] * (1.0 / total[HD : HD + 1])
        for u in range(WT):
            write(row * WT + u, out[:, u * TILE : (u + 1) * TILE].T.astype(jnp.bfloat16))

    def rows(i, carry):
        at = [i * 2 + j for j in range(2)]
        peaks = [score(r, s_ref) for r, s_ref in zip(at, score_refs)]
        for r, s_ref, peak in zip(at, score_refs, peaks):
            combine(r, s_ref, peak)
        return carry

    lax.fori_loop(0, HT // 2, rows, 0)


def attend_row(queries, kv_ref, frames, head, table):
    entry = ROW_TABLE + head * ROW_ENTRIES
    columns = [table[entry + c] for c in range(WT)]
    blocks = [(f, c, columns[c] + table[entry + WT + f]) for f in frames for c in range(WT)]
    scores = []
    peak = None
    for f, c, bias in blocks:
        s = lax.dot_general(
            kv_ref[f, c, head, 0], queries, (((1,), (1,)), ((), ())), preferred_element_type=jnp.float32
        )
        scores.append(s)
        top = block_max(s) + bias
        peak = top if peak is None else jnp.maximum(peak, top)
    peak = jnp.max(peak, axis=0, keepdims=True) * LOG2_SCALE
    weights = jnp.concatenate(
        [jnp.exp2(s * LOG2_SCALE + (bias - peak)) for s, (_, _, bias) in zip(scores, blocks)], axis=0
    ).astype(jnp.bfloat16)
    values = jnp.concatenate([kv_ref[f, c, head, 1] for f, c, _ in blocks], axis=1)
    values = jnp.concatenate([values, jnp.ones((16, values.shape[1]), jnp.bfloat16)], axis=0)
    total = jnp.dot(values, weights, preferred_element_type=jnp.float32)
    return (total[:HD] * (1.0 / total[HD : HD + 1])).T.astype(jnp.bfloat16)


def exchange_kernel(
    halves, wide, frame_total,
    table_hbm, kv_stage, q_stage,
    out,
    table, kv_wide, kv_near, kv_row, q_near, q_row, o_stage, o_row, scores_a, scores_b,
    table_sem, kv_send, kv_recv, q_send, q_recv, halo_send, halo_recv, o_send, o_recv, own_sem,
    row_send, row_recv, side_send, side_recv, row_sem,
):
    full, half = halves // 2, halves % 2
    slots = full + half
    row_base = halves * HALF
    row_heads = H - row_base
    me = lax.axis_index("head")
    seq = lax.axis_index("seq")
    later = lax.rem(seq + 1, frame_total)
    earlier = lax.rem(seq + frame_total - 1, frame_total)
    column = lax.rem(me, WT)
    chip = me // WT
    sibling = me + 1 - 2 * column
    spot = column * HALF + chip

    table_load = pltpu.make_async_copy(table_hbm, table, table_sem.at[0])
    table_load.start()

    def peer(d):
        return lax.rem(me + d, TILES)

    barrier = pltpu.get_barrier_semaphore()
    for d in range(1, TILES):
        pl.semaphore_signal(barrier, inc=1, device_id=(seq, peer(d)), device_id_type=MESH)
    for frame in (later, earlier):
        pl.semaphore_signal(barrier, inc=1, device_id=(frame, me), device_id_type=MESH)
    pl.semaphore_wait(barrier, TILES - 1 + 2)

    def remote(src, dst, send, recv, frame, group):
        return pltpu.make_async_remote_copy(
            src_ref=src, dst_ref=dst, send_sem=send, recv_sem=recv,
            device_id=(frame, group), device_id_type=MESH,
        )

    def wide_tile(s, t):
        return kv_wide.at[s, 1, t]

    def near_tile(s, t):
        return kv_near.at[s - wide, 0, t]

    def send_kv_tile(s, place, tile_at, group):
        src = kv_stage.at[s * TILES + place]
        remote(src, tile_at(s, me), kv_send.at[s], kv_recv.at[s], seq, group).start()

    def send_q_tile(s, place, group):
        src = q_stage.at[s * TILES + place]
        remote(src, q_near.at[s, me], q_send.at[s], q_recv.at[s], seq, group).start()

    def own_kv(s, tile_at):
        return pltpu.make_async_copy(kv_stage.at[s * TILES + spot], tile_at(s, me), own_sem.at[0, s])

    def own_q(s):
        return pltpu.make_async_copy(q_stage.at[s * TILES + spot], q_near.at[s, me], own_sem.at[1, s])

    def place_of(group):
        return lax.rem(group, WT) * HALF + group // WT

    def send_kv(s, tile_at):
        for d in range(1, TILES):
            group = peer(d)
            send_kv_tile(s, place_of(group), tile_at, group)
        own_kv(s, tile_at).start()

    def send_q(s):
        for d in range(1, TILES):
            group = peer(d)
            send_q_tile(s, place_of(group), group)
        own_q(s).start()

    def send_half(s):
        for i in range(1, HALF):
            place = lax.rem(chip + i, HALF)
            send_kv_tile(s, place, near_tile, place * WT)
        for i in range(1, HALF):
            place = lax.rem(chip + i, HALF)
            send_q_tile(s, place, place * WT)

        @pl.when(column == 0)
        def _():
            own_kv(s, near_tile).start()
            own_q(s).start()

        @pl.when(column == 1)
        def _():
            send_kv_tile(s, chip, near_tile, sibling)
            send_q_tile(s, chip, sibling)

    def halo_copies(s):
        return [
            remote(
                kv_wide.at[s, 1], kv_wide.at[s, 2 * side],
                halo_send.at[s, side], halo_recv.at[s, side], frame, me,
            )
            for side, frame in enumerate((later, earlier))
        ]

    row_parts = row_heads // HALF

    def part_of(f, part):
        return kv_row.at[f, column, pl.ds(part * HALF, HALF)]

    def staged_part(part):
        return kv_stage.at[pl.ds(row_base + part * HALF, HALF)]

    def row_halo(part):
        return [
            remote(
                staged_part(part), part_of(2 * side, part),
                row_send.at[part, side], row_recv.at[part, side], frame, me,
            )
            for side, frame in enumerate((later, earlier))
        ]

    def to_sibling(f, part):
        return remote(
            staged_part(part) if f == 1 else part_of(f, part), part_of(f, part),
            side_send.at[f, part], side_recv.at[f, part], seq, sibling,
        )

    def own_row():
        rows = pl.ds(row_base, row_heads)
        return [
            pltpu.make_async_copy(kv_stage.at[rows], kv_row.at[1, column], row_sem.at[0]),
            pltpu.make_async_copy(q_stage.at[rows], q_row, row_sem.at[1]),
        ]

    def start_wide_kv(s, carry):
        send_kv(s, wide_tile)
        return carry

    def start_q(s, carry):
        send_q(s)
        return carry

    def start_near(s, carry):
        send_kv(s, near_tile)
        send_q(s)
        return carry

    def forward(s, carry):
        bytes_of(kv_wide.at[s, 1, pl.ds(0, TILES - 1)], kv_recv.at[s]).wait()
        own_kv(s, wide_tile).wait()
        for copy in halo_copies(s):
            copy.start()
        return carry

    send_kv(0, wide_tile)
    if row_heads:
        for copy in row_halo(0):
            copy.start()
    lax.fori_loop(1, wide, start_wide_kv, 0)
    for part in range(row_parts):
        to_sibling(1, part).start()
    if row_heads:
        for copy in own_row():
            copy.start()
    lax.fori_loop(0, wide, start_q, 0)
    if full > wide:
        lax.fori_loop(wide, full, start_near, 0)
    if half:
        send_half(full)
    lax.fori_loop(0, 2, forward, 0)
    if row_heads:
        for side, copy in enumerate(row_halo(0)):
            copy.wait_recv()
            to_sibling(2 * side, 0).start()
    lax.fori_loop(2, wide, forward, 0)
    if row_heads:
        for copy in row_halo(1):
            copy.start()

    def row_pairs(part, frames):
        def heads(i, carry):
            for j in range(2):
                head = part * HALF + i * 2 + j
                o_row[head] = attend_row(q_row[head], kv_row, frames, head, table)
            return carry

        lax.fori_loop(0, HALF // 2, heads, 0)

    def row_part(part, frames):
        for f in frames:
            to_sibling(f, part).wait_recv()
        row_pairs(part, frames)

    table_load.wait()
    if row_heads:
        for copy in own_row():
            copy.wait()
        row_part(0, (0, 1, 2))
    if row_parts > 2:
        row_part(2, (1,))

    def attend_slot(s, kv_ref, first_frame):
        bytes_of(q_near.at[s, pl.ds(0, TILES - 1)], q_recv.at[s]).wait()
        own_q(s).wait()

        def write(t, tile):
            o_stage[s, t] = tile

        attend(q_near.at[s], kv_ref, (scores_a, scores_b), write, table, s, first_frame)
        position = s * TILES + spot
        for d in range(1, TILES):
            group = peer(d)
            remote(
                o_stage.at[s, group], out.at[position], o_send.at[s], o_recv.at[s], seq, group
            ).start()
        pltpu.make_async_copy(o_stage.at[s, me], out.at[position], own_sem.at[2, s]).start()

    def wide_slot(s, carry):
        for copy in halo_copies(s):
            copy.wait_recv()
        attend_slot(s, kv_wide.at[s], 0)
        return carry

    def near_slot(s, carry):
        bytes_of(kv_near.at[s - wide, 0, pl.ds(0, TILES - 1)], kv_recv.at[s]).wait()
        own_kv(s, near_tile).wait()
        attend_slot(s, kv_near.at[s - wide], 1)
        return carry

    near = slots - wide
    first = max(wide - near, 0)

    def pair(j, carry):
        if half:
            @pl.when((wide + j < full) | (column == 0))
            def _():
                near_slot(wide + j, 0)
        else:
            near_slot(wide + j, 0)
        wide_slot(first + j, 0)
        return carry

    if first:
        lax.fori_loop(0, first, wide_slot, 0)
    if near:
        lax.fori_loop(0, near, pair, 0)

    if row_heads:
        for side, copy in enumerate(row_halo(1)):
            copy.wait_recv()
            to_sibling(2 * side, 1).start()
        row_part(1, (0, 1, 2))
        pltpu.make_async_copy(o_row, out.at[pl.ds(row_base, row_heads)], row_sem.at[2]).start()

    def own_out(s):
        return pltpu.make_async_copy(o_stage.at[s, me], out.at[s * TILES + spot], own_sem.at[2, s])

    def sent_inputs(s, count):
        bytes_of(kv_stage.at[pl.ds(s * TILES, count)], kv_send.at[s]).wait()
        bytes_of(q_stage.at[pl.ds(s * TILES, count)], q_send.at[s]).wait()

    def got_outputs(s, count):
        bytes_of(out.at[pl.ds(s * TILES, count)], o_recv.at[s]).wait()

    def sent_outputs(s):
        own_out(s).wait()
        bytes_of(o_stage.at[s, pl.ds(0, TILES - 1)], o_send.at[s]).wait()

    def finish(s, carry):
        sent_inputs(s, TILES - 1)
        sent_outputs(s)
        got_outputs(s, TILES - 1)
        return carry

    def finish_halo(s, carry):
        for copy in halo_copies(s):
            copy.wait_send()
        return carry

    lax.fori_loop(0, wide, finish_halo, 0)
    for part in range(min(row_parts, 2)):
        for copy in row_halo(part):
            copy.wait_send()
    for part in range(row_parts):
        for f in (0, 1, 2) if part < 2 else (1,):
            to_sibling(f, part).wait_send()
    if row_heads:
        pltpu.make_async_copy(o_row, out.at[pl.ds(row_base, row_heads)], row_sem.at[2]).wait()
    if half:
        @pl.when(column == 0)
        def _():
            sent_inputs(full, HALF - 1)
            sent_outputs(full)
            got_outputs(full, HALF - 1)

        @pl.when(column == 1)
        def _():
            sent_inputs(full, HALF)
            got_outputs(full, HALF)
    lax.fori_loop(0, full, finish, 0)


def exchange(halves, wide, collective_id, frame_total, table, kv_stage, q_stage):
    slots = (halves + 1) // 2
    near = max(slots - wide, 1)
    row_heads = max(H - halves * HALF, 1)
    hbm = pl.BlockSpec(memory_space=pl.ANY)
    bf16 = jnp.bfloat16
    tile = (TILE, HD)
    dma = pltpu.SemaphoreType.DMA
    scores = pltpu.VMEM((FRAMES * TILES * TILE, WT * TILE), jnp.float32)
    return pl.pallas_call(
        functools.partial(exchange_kernel, halves, wide, frame_total),
        out_shape=jax.ShapeDtypeStruct((H,) + tile, bf16),
        in_specs=[hbm] * 3,
        out_specs=hbm,
        scratch_shapes=[
            pltpu.SMEM((TABLE,), jnp.float32),
            pltpu.VMEM((wide, FRAMES, TILES, 2) + tile, bf16),
            pltpu.VMEM((near, 1, TILES, 2) + tile, bf16),
            pltpu.VMEM((FRAMES, WT, row_heads, 2) + tile, bf16),
            pltpu.VMEM((slots, TILES) + tile, bf16),
            pltpu.VMEM((row_heads,) + tile, bf16),
            pltpu.VMEM((slots, TILES) + tile, bf16),
            pltpu.VMEM((row_heads,) + tile, bf16),
            scores, scores,
            dma((1,)),
            dma((slots,)), dma((slots,)), dma((slots,)), dma((slots,)),
            dma((wide, 2)), dma((wide, 2)),
            dma((slots,)), dma((slots,)), dma((3, slots)),
            dma((2, 2)), dma((2, 2)),
            dma((FRAMES, FRAMES)), dma((FRAMES, FRAMES)),
            dma((3,)),
        ],
        compiler_params=pltpu.CompilerParams(
            collective_id=collective_id, has_side_effects=True, vmem_limit_bytes=60 << 20
        ),
        name=f"exchange_{halves}_{wide}",
    )(table, kv_stage, q_stage)


def power(exponent):
    return jnp.where(exponent > 0, 2.0, jnp.where(exponent < 0, 0.5, 1.0)).astype(jnp.float32)


def prepare_kernel(
    frame_total,
    extents, q_exp, k_exp, v_exp, q_data, k_data, v_data,
    table, place, plan, kv_out, q_out,
    order, q_in, k_in, v_in, kv_stage, q_stage, in_sem, out_sem,
):
    loads = [
        pltpu.make_async_copy(src, dst, in_sem.at[i])
        for i, (src, dst) in enumerate(((k_data, k_in), (v_data, v_in), (q_data, q_in)))
    ]
    for load in loads:
        load.start()

    zero = jnp.int32(0)
    one = jnp.int32(1)

    def flag(condition):
        return jnp.where(condition, one, zero)

    reach = [flag(extents[0, h] >= 1) for h in range(H)]
    flat = [flag(extents[1, h] <= 0) for h in range(H)]
    reaching = sum(reach, zero)
    flat_reaching = sum((r * f for r, f in zip(reach, flat)), zero)
    row_reaching = jnp.minimum(flat_reaching, ROW_REACH)
    row_most = row_reaching + sum(flat, zero) - flat_reaching
    fits = flag(reaching - row_reaching <= PLANS[0][1] * TILES)
    twelve = fits * flag(row_most >= ROW_HEADS)
    eight = fits * flag(row_most >= TILES) * (1 - twelve)
    row_count = twelve * ROW_HEADS + eight * TILES
    row_reaching = flag(row_count > 0) * row_reaching
    row_base = H - row_count
    plan[0] = jnp.where(twelve > 0, 0, jnp.where(eight > 0, 1, 2))
    next_reach, next_rest = zero, reaching - row_reaching
    next_row_reach, next_row_rest = zero, row_reaching
    for h in range(H):
        row_index = jnp.where(reach[h] > 0, next_row_reach, next_row_rest)
        row_end = jnp.where(reach[h] > 0, row_reaching, row_count)
        in_row = flat[h] * flag(row_index < row_end)
        outside = 1 - in_row
        other = jnp.where(reach[h] > 0, next_reach, next_rest)
        position = jnp.where(in_row > 0, row_base + row_index, other)
        next_row_reach += in_row * reach[h]
        next_row_rest += in_row * (1 - reach[h])
        next_reach += outside * reach[h]
        next_rest += outside * (1 - reach[h])
        order[position] = h
        place[h] = position
    me = lax.axis_index("head")
    seq = lax.axis_index("seq")
    column = lax.rem(me, WT)
    spot = column * HALF + me // WT

    def within(condition):
        return jnp.where(condition, 0.0, NEG).astype(jnp.float32)

    def beside(head, f):
        inside = (seq + f - 1 >= 0) & (seq + f - 1 < frame_total)
        return within((extents[0, head] >= abs(f - 1)) & inside)

    for s in range(SLOTS):
        head = order[s * TILES + spot]
        entry = s * ENTRIES
        for r in range(HT):
            for t in range(HT):
                table[entry + r * HT + t] = within(extents[1, head] >= abs(r - t))
        for c in range(WT):
            table[entry + HT * HT + c] = within(extents[2, head] >= c)
        for f in range(FRAMES):
            table[entry + HT * HT + WT + f] = beside(head, f)
    for i in range(ROW_HEADS):
        head = order[jnp.minimum(row_base + i, H - 1)]
        entry = ROW_TABLE + i * ROW_ENTRIES
        for c in range(WT):
            table[entry + c] = within(extents[2, head] >= jnp.abs(column - c))
        for f in range(FRAMES):
            table[entry + WT + f] = beside(head, f)


    def scaled(ref, exps, head):
        columns = pl.ds(pl.multiple_of(head * HD, HD), HD)
        return (ref[:, columns].astype(jnp.float32) * power(exps[0, head])).astype(jnp.bfloat16)

    def slot_of(s):
        return pl.ds(s * TILES, TILES)

    def kv_copy(s, which):
        rows = slot_of(s)
        return pltpu.make_async_copy(
            kv_stage.at[rows, which], kv_out.at[rows, which], out_sem.at[which, s]
        )

    def q_copy(s):
        return pltpu.make_async_copy(q_stage.at[slot_of(s)], q_out.at[slot_of(s)], out_sem.at[2, s])

    def stage_keys(s, carry):
        for p in range(TILES):
            kv_stage[s * TILES + p, 0] = scaled(k_in, k_exp, order[s * TILES + p])
        kv_copy(s, 0).start()
        return carry

    def stage_values(s, carry):
        for p in range(TILES):
            kv_stage[s * TILES + p, 1] = scaled(v_in, v_exp, order[s * TILES + p]).T
        kv_copy(s, 1).start()
        return carry

    def stage_queries(s, carry):
        for p in range(TILES):
            q_stage[s * TILES + p] = scaled(q_in, q_exp, order[s * TILES + p])
        q_copy(s).start()
        return carry

    for load, stage in zip(loads, (stage_keys, stage_values, stage_queries)):
        load.wait()
        lax.fori_loop(0, SLOTS, stage, 0)
    for s in range(SLOTS):
        kv_copy(s, 0).wait()
        kv_copy(s, 1).wait()
        q_copy(s).wait()


def prepare(frame_total, extents, q_exp, k_exp, v_exp, q_data, k_data, v_data):
    smem = pl.BlockSpec(memory_space=pltpu.SMEM)
    hbm = pl.BlockSpec(memory_space=pl.ANY)
    bf16 = jnp.bfloat16
    kv = (H, 2, TILE, HD)
    q = (H, TILE, HD)
    whole = pltpu.VMEM((TILE, H * HD), bf16)
    return pl.pallas_call(
        functools.partial(prepare_kernel, frame_total),
        out_shape=(
            jax.ShapeDtypeStruct((TABLE,), jnp.float32),
            jax.ShapeDtypeStruct((H,), jnp.int32),
            jax.ShapeDtypeStruct((1,), jnp.int32),
            jax.ShapeDtypeStruct(kv, bf16),
            jax.ShapeDtypeStruct(q, bf16),
        ),
        in_specs=[smem] * 4 + [hbm] * 3,
        out_specs=(smem, smem, smem, hbm, hbm),
        scratch_shapes=[
            pltpu.SMEM((H,), jnp.int32),
            whole, whole, whole,
            pltpu.VMEM(kv, bf16),
            pltpu.VMEM(q, bf16),
            pltpu.SemaphoreType.DMA((3,)),
            pltpu.SemaphoreType.DMA((3, SLOTS)),
        ],
        compiler_params=pltpu.CompilerParams(vmem_limit_bytes=60 << 20),
        name="prepare",
    )(extents, q_exp, k_exp, v_exp, q_data, k_data, v_data)


def restore_kernel(place, tiles, out, held, in_sem, out_sem):
    parts = out_sem.shape[0]
    heads = H // parts

    def block(ref, i):
        return ref.at[:, pl.ds(i * heads * HD, heads * HD)]

    for h in range(H):
        columns = held.at[:, pl.ds(h * HD, HD)]
        pltpu.make_async_copy(tiles.at[place[h]], columns, in_sem.at[h // heads]).start()
    for i in range(parts):
        bytes_of(block(held, i), in_sem.at[i]).wait()
        pltpu.make_async_copy(block(held, i), block(out, i), out_sem.at[i]).start()
    for i in range(parts):
        pltpu.make_async_copy(block(held, i), block(out, i), out_sem.at[i]).wait()


def restore(place, tiles):
    hbm = pl.BlockSpec(memory_space=pl.ANY)
    return pl.pallas_call(
        restore_kernel,
        out_shape=jax.ShapeDtypeStruct((TILE, H * HD), jnp.bfloat16),
        in_specs=[pl.BlockSpec(memory_space=pltpu.SMEM), hbm],
        out_specs=hbm,
        scratch_shapes=[
            pltpu.VMEM((TILE, H * HD), jnp.bfloat16),
            pltpu.SemaphoreType.DMA((4,)),
            pltpu.SemaphoreType.DMA((4,)),
        ],
        compiler_params=pltpu.CompilerParams(vmem_limit_bytes=60 << 20),
        name="restore",
    )(place, tiles)


def on_device(frame_total, q_data, k_data, v_data, q_exp, k_exp, v_exp, extents):
    table, place, plan, kv_stage, q_stage = prepare(
        frame_total, extents.T, q_exp, k_exp, v_exp, q_data, k_data, v_data
    )
    branches = [
        functools.partial(exchange, halves, wide, i, frame_total)
        for i, (halves, wide) in enumerate(PLANS)
    ]
    tiles = lax.switch(plan[0], branches, table, kv_stage, q_stage)
    return restore(place, tiles)


def solution(mesh):
    rows = P(("seq", "head"), None)
    return jax.shard_map(
        functools.partial(on_device, mesh.shape["seq"]),
        mesh=mesh,
        in_specs=(rows,) * 6 + (P(),),
        out_specs=rows,
        check_vma=False,
    )
```

time: 127 us -> 109 us (0.86)
  Pallas kernels: 125 us -> 107 us
    pallas_call x1, Pallas kernels: 49.4 us -> 2.82 us  [restore(): pl.pallas_call(restore_kernel, out_shape=jax.ShapeDtypeStruct((TILE, H *...]
    pallas_call x1, Pallas kernels: 70.3 us -> 99 us  [exchange(): pl.pallas_call(functools.partial(exchange_kernel, halves, wide, frame_tot...]
where the time goes in v3:
time: 109 us
  Pallas kernels  107 us (98%)
    pallas_call x1, Pallas kernels, exchange(): pl.pallas_call(functools.partial(exchange_kernel, halves, wide, frame_tot...  99 us
    pallas_call x1, Pallas kernels, prepare(): pl.pallas_call(functools.partial(prepare_kernel, frame_total), out_shape=...  5.68 us
    pallas_call x1, Pallas kernels, restore(): pl.pallas_call(restore_kernel, out_shape=jax.ShapeDtypeStruct((TILE, H *...  2.82 us

profile of v3, /device:TPU:1, one launch (start us, length us, event | category | flops | bytes accessed | tf_op | source)
XLA Modules:
  0.0 108.7 jit_solution(520969431834256957)
XLA Ops:
  0.0 5.7 %prepare.1 = (f32[186]{0:T(256)S(1)}, s32[48]{0:T(128)}, s32[1]{0:T(128)}, bf16[48,2,128,128]{3,2,1,0:T(8,128)(2,1)S(1)}, bf16[48,128,128]{2,1,0:T(8,128)(2,1)}) custom-call(s32[3,48]{1,0:T(4,128)} %bitcast.2, s32[1,48]{1,0:T(1,128)} %q_exp.1, s32[1,48]{1,0:T(1,128)} %k_exp.1, s32[1,48]{1,0:T(1,128)} %v_exp.1, bf16[128,6144]{1,0:T(8,128)(2,1)} %q_data.1, ...), custom_call_target="tpu_custom_call" | custom-call | tf_op jit(solution)/shard_map/prepare/pallas_call | solution.py:599
  6.3 99.4 %conditional.1 = (bf16[48,128,128]{2,1,0:T(8,128)(2,1)}) conditional(s32[]{:T(128)} %bitcast.1, (f32[186]{0:T(256)S(1)}, bf16[48,2,128,128]{3,2,1,0:T(8,128)(2,1)S(1)}, bf16[48,128,128]{2,1,0:T(8,128)(2,1)}) %tuple.14, (f32[186]{0:T(256)S(1)}, bf16[48,2,128,128]{3,2,1,0:T(8,128)(2,1)S(1)}, ...), branch_computations={%region_0.0_spmd, %region_1.0_spmd, %region_2.0_spmd} | conditional | bytes 8 | solution.py:665
  6.5 99.0 %exchange_12_6.1 = bf16[48,128,128]{2,1,0:T(8,128)(2,1)} custom-call(f32[186]{0:T(256)S(1)} %get-tuple-element.33.table_hbm, bf16[48,2,128,128]{3,2,1,0:T(8,128)(2,1)S(1)} %get-tuple-element.34.kv_stage, bf16[48,128,128]{2,1,0:T(8,128)(2,1)} %get-tuple-element.35.q_stage), custom_call_target="tpu_custom_call" | custom-call | tf_op jit(solution)/shard_map/cond/branch_2_fun/exchange_12_6/pallas_call | solution.py:437
  105.7 2.8 %restore.1 = bf16[128,6144]{1,0:T(8,128)(2,1)} custom-call(s32[48]{0:T(128)} %get-tuple-element.41.place, bf16[48,128,128]{2,1,0:T(8,128)(2,1)} %get-tuple-element.46.tiles), custom_call_target="tpu_custom_call" | custom-call | tf_op jit(solution)/shard_map/restore/pallas_call | solution.py:642
